TPU v7x, 32 devices: a whole 2x2x4 slice. The times are simulated.
32 devices in a mesh: blk: 16 (over z, y, x), rep: 2 (over core).
Axes of the slice: x: 2, y: 2, z: 4, core: 2. Of those that a mesh axis runs over, the one named last changes fastest.
Arguments:
- counts: int32 [32, 1024, 1024], P(('blk', 'rep')), may hold values from 0 to 127
- tile_list: int32 [32, 2], replicated, may hold values from 0 to 15, as said below
- owner_map: int32 [2, 16], replicated, may hold values from 0 to 15, each once within a row
- embed: float32 [2, 16384, 256], P('rep', 'blk'), may hold values from -0.375 to 0.375
- accum: float32 [2, 16384, 256], P('rep', 'blk'), may hold values from 1 to 30
- margins: bfloat16 [2, 16384], P('rep', 'blk'), may hold values from -1 to 2
Outputs:
- new_embed: float32 [2, 16384, 256], P('rep', 'blk')
- new_accum: float32 [2, 16384, 256], P('rep', 'blk')
Inputs may be any that keep to these rules, and one draw needn't show every extreme that they name: `tile_list`: each row block id and each column block id is named by at least one device.
All inputs are finite; a program needn't handle non-finite values.
Results may differ from a plain program's by a relative error of at most 0.0046.
Values may be sent and summed in bfloat16 or wider, within the bound.
No kernel may reach another device: no remote copies, remote signals or barrier semaphores. Data moves between devices by JAX's collectives and lax.ppermute only.
A program may use at most 64 MiB of HBM per device.

v0:
```python
import jax
import jax.numpy as jnp
from jax import lax
from jax.sharding import PartitionSpec as P

learn_rate = 0.05
conf_base = 0.1
conf_scale = 0.25


def cell_gradient(tile_counts, scores, row_offset, col_offset):
    present = tile_counts > 0
    counted = jnp.maximum(tile_counts, 1).astype(jnp.float32)
    offsets = row_offset.astype(jnp.float32)[:, None] + col_offset.astype(jnp.float32)[None, :]
    confidence = conf_base + conf_scale * jnp.sqrt(counted)
    fitted = confidence * (scores - jnp.log(counted) + offsets)
    hinge = jax.nn.sigmoid(scores + offsets)
    return jnp.where(present, fitted, hinge).astype(jnp.bfloat16)


def per_device(counts, tile_list, owner_map, embed, accum, margins):
    owners = lax.axis_size("blk")
    plane_index = lax.axis_index("rep")
    block_rows = embed.shape[1]
    embed_width = embed.shape[2]
    piece_rows = block_rows // owners
    own_vectors = embed[0].astype(jnp.bfloat16).reshape(owners, piece_rows, embed_width)
    own_offsets = margins[0].reshape(owners, piece_rows)
    holdings, held_offsets = (
        lax.all_to_all(own_vectors, "blk", split_axis=0, concat_axis=0, tiled=True),
        lax.all_to_all(own_offsets, "blk", split_axis=0, concat_axis=0, tiled=True),
    )
    wanted = jnp.take(tile_list, plane_index, axis=1)
    slot_of = jnp.take(jnp.take(owner_map, plane_index, axis=0), wanted)
    outgoing = jnp.take(holdings, slot_of, axis=0)
    outgoing_offsets = jnp.take(held_offsets, slot_of, axis=0)
    requests = outgoing.shape[0]
    arrived, arrived_offsets = (
        lax.all_to_all(outgoing, ("blk", "rep"), split_axis=0, concat_axis=0, tiled=True),
        lax.all_to_all(outgoing_offsets, ("blk", "rep"), split_axis=0, concat_axis=0, tiled=True),
    )
    arrived = arrived.reshape(owners, 2, piece_rows, embed_width)
    arrived_offsets = arrived_offsets.reshape(owners, 2, piece_rows)
    row_vectors = arrived[:, 0].reshape(block_rows, embed_width)
    col_vectors = arrived[:, 1].reshape(block_rows, embed_width)
    row_offset = arrived_offsets[:, 0].reshape(block_rows)
    col_offset = arrived_offsets[:, 1].reshape(block_rows)
    scores = lax.dot_general(
        row_vectors, col_vectors, (((1,), (1,)), ((), ())), preferred_element_type=jnp.float32
    )
    cell_grad = cell_gradient(counts[0], scores, row_offset, col_offset)
    row_gradient = jnp.dot(cell_grad, col_vectors, preferred_element_type=jnp.float32)
    col_gradient = lax.dot_general(
        cell_grad, row_vectors, (((0,), (0,)), ((), ())), preferred_element_type=jnp.float32
    )
    partials = jnp.stack(
        (
            row_gradient.reshape(owners, piece_rows, embed_width),
            col_gradient.reshape(owners, piece_rows, embed_width),
        ),
        axis=1,
    )
    returned = lax.all_to_all(
        partials.reshape(requests, piece_rows, embed_width),
        ("blk", "rep"),
        split_axis=0,
        concat_axis=0,
        tiled=True,
    )
    selector = (slot_of[None, :] == jnp.arange(owners, dtype=jnp.int32)[:, None]).astype(
        jnp.float32
    )
    summed = jnp.dot(
        selector,
        returned.reshape(requests, piece_rows * embed_width),
        precision=lax.Precision.HIGHEST,
        preferred_element_type=jnp.float32,
    )
    gradient = lax.all_to_all(
        summed.reshape(owners, piece_rows, embed_width),
        "blk",
        split_axis=0,
        concat_axis=0,
        tiled=True,
    ).reshape(block_rows, embed_width)
    new_accum = accum[0] + gradient * gradient
    new_embed = embed[0] - learn_rate * gradient / jnp.sqrt(new_accum)
    return (new_embed[None], new_accum[None])


def solution(mesh):
    in_specs = (
        P(("blk", "rep"), None, None),
        P(),
        P(),
        P("rep", "blk", None),
        P("rep", "blk", None),
        P("rep", "blk"),
    )
    out_specs = (P("rep", "blk", None), P("rep", "blk", None))
    return jax.shard_map(
        per_device, mesh=mesh, in_specs=in_specs, out_specs=out_specs, check_vma=False
    )
```

profile of v0, /device:TPU:0, one launch (start us, length us, event | category | flops | bytes accessed | tf_op | source)
XLA Modules:
  0.0 173.0 jit_solution(9770106951563197902)
XLA Ops:
  0.6 0.7 reduce
  1.3 0.7 all_to_all.32
  2.0 8.3 %all-to-all-start.2 = ((bf16[16,1,64]{2,1,0:T(2,128)(2,1)}), bf16[16,1,64]{2,1,0:T(2,128)(2,1)S(1)}, u32[]{:S(2)}, u32[]{:S(2)}) async-start(bf16[16,1,64]{2,1,0:T(2,128)(2,1)} %all_to_all.32), calls=%async_computation.2 | async-start | bytes 16384 | tf_op jit(solution)/shard_map/all_to_all | solution.py:31
  10.3 0.7 fusion.16
  11.0 2.1 %convert_element_type.36 = bf16[1,1024,256]{2,1,0:T(8,128)(2,1)} convert(f32[1,1024,256]{2,1,0:T(8,128)} %param.9) | non-fusion elementwise | flops 262144 | bytes 1572864 | tf_op jit(solution)/shard_map/convert_element_type | solution.py:27
  13.1 4.4 %all-to-all-done.2 = bf16[16,1,64]{2,1,0:T(2,128)(2,1)S(1)} async-done(((bf16[16,1,64]{2,1,0:T(2,128)(2,1)}), bf16[16,1,64]{2,1,0:T(2,128)(2,1)S(1)}, u32[]{:S(2)}, u32[]{:S(2)}) %all-to-all-start.2) | async-done | bytes 2080 | tf_op jit(solution)/shard_map/all_to_all | solution.py:31
  17.5 3.6 %all-to-all-start = ((bf16[16,64,256]{2,1,0:T(8,128)(2,1)}), bf16[16,64,256]{2,1,0:T(8,128)(2,1)S(1)}, u32[]{:S(2)}, u32[]{:S(2)}) async-start(bf16[16,64,256]{2,1,0:T(8,128)(2,1)} %bitcast.6), calls=%async_computation | async-start | bytes 1048576 | tf_op jit(solution)/shard_map/all_to_all | solution.py:30
  21.1 0.7 fusion.18
  21.8 0.7 gather_fusion
  23.2 0.6 copy.20
  23.9 11.2 %all-to-all-done = bf16[16,64,256]{2,1,0:T(8,128)(2,1)S(1)} async-done(((bf16[16,64,256]{2,1,0:T(8,128)(2,1)}), bf16[16,64,256]{2,1,0:T(8,128)(2,1)S(1)}, u32[]{:S(2)}, u32[]{:S(2)}) %all-to-all-start) | async-done | bytes 524320 | tf_op jit(solution)/shard_map/all_to_all | solution.py:30
  35.1 2.8 %all-to-all-start.3 = ((bf16[32,1,64]{2,1,0:T(2,128)(2,1)}), bf16[32,1,64]{2,1,0:T(2,128)(2,1)S(1)}, u32[]{:S(2)}, u32[]{:S(2)}) async-start(bf16[32,1,64]{2,1,0:T(2,128)(2,1)} %copy.20), calls=%async_computation.3 | async-start | bytes 32768 | tf_op jit(solution)/shard_map/all_to_all | solution.py:40
  38.5 1.1 broadcast_select_fusion
  39.7 5.3 %all-to-all-done.3 = bf16[32,1,64]{2,1,0:T(2,128)(2,1)S(1)} async-done(((bf16[32,1,64]{2,1,0:T(2,128)(2,1)}), bf16[32,1,64]{2,1,0:T(2,128)(2,1)S(1)}, u32[]{:S(2)}, u32[]{:S(2)}) %all-to-all-start.3) | async-done | bytes 4128 | tf_op jit(solution)/shard_map/all_to_all | solution.py:40
  45.0 2.6 %all-to-all-start.1 = ((bf16[32,64,256]{2,1,0:T(8,128)(2,1)}), bf16[32,64,256]{2,1,0:T(8,128)(2,1)S(1)}, u32[]{:S(2)}, u32[]{:S(2)}) async-start(bf16[32,64,256]{2,1,0:T(8,128)(2,1)} %broadcast_select_fusion), calls=%async_computation.1 | async-start | bytes 2097152 | tf_op jit(solution)/shard_map/all_to_all | solution.py:39
  47.8 26.0 %all-to-all-done.1 = bf16[32,64,256]{2,1,0:T(8,128)(2,1)S(1)} async-done(((bf16[32,64,256]{2,1,0:T(8,128)(2,1)}), bf16[32,64,256]{2,1,0:T(8,128)(2,1)S(1)}, u32[]{:S(2)}, u32[]{:S(2)}) %all-to-all-start.1) | async-done | bytes 1048608 | tf_op jit(solution)/shard_map/all_to_all | solution.py:39
  73.9 5.4 %fusion.2 = bf16[1024,1024]{1,0:T(8,128)(2,1)S(1)} fusion(s32[1,1024,1024]{2,1,0:T(8,128)} %param.6, f32[1024]{0:T(1024)S(1)} %reshape.241, f32[1024]{0:T(1024)S(1)} %reshape.240, bf16[1024,256]{1,0:T(8,128)(2,1)S(1)} %bitcast.79, bf16[1024,256]{1,0:T(8,128)(2,1)S(1)} %bitcast.81), kind=kOutput, calls=%fused_computation.7 | convolution fusion | flops 552599552 | bytes 7348224 | tf_op jit(solution)/shard_map/dot_general | solution.py:48
  79.3 2.6 %copy.21 = bf16[1024,1024]{1,0:T(8,128)(2,1)} copy(bf16[1024,1024]{0,1:T(8,128)(2,1)S(1)} %bitcast.71) | data formatting | bytes 4194304 | tf_op jit(solution)/shard_map/dot_general | solution.py:53
  81.9 0.7 convolution_bitcast_fusion.1
  82.6 2.3 %convolution_bitcast_fusion = f32[16,1,64,256]{3,2,0,1:T(8,128)S(1)} fusion(bf16[16,64,1024]{2,1,0:T(8,128)(2,1)} %bitcast.73, bf16[1024,256,1]{1,0,2:T(8,128)(2,1)S(1)} %bitcast.80), kind=kOutput, calls=%fused_computation.17 | convolution fusion | flops 536870912 | bytes 3670016 | tf_op jit(solution)/shard_map/dot_general | solution.py:53
  85.4 52.1 %all_to_all.39 = f32[32,64,256]{2,1,0:T(8,128)S(1)} all-to-all(f32[32,64,256]{2,1,0:T(8,128)S(1)} %bitcast.75), channel_id=1, replica_groups=mesh['blk'=16,'rep'=2] {'blk','rep'}, dimensions={0} | all-to-all | bytes 4194304 | tf_op jit(solution)/shard_map/all_to_all | solution.py:63
  137.4 2.0 %fusion.7 = f32[16,64,256]{2,0,1:T(8,128)S(1)} fusion(s32[32]{0:T(128)S(1)} %get-tuple-element.29, f32[4,8,64,256]{3,2,1,0:T(8,128)S(1)} %bitcast.74), kind=kOutput, calls=%fused_computation.13 | convolution fusion | flops 100663808 | bytes 3145856 | tf_op jit(solution)/shard_map/dot_general | solution.py:73
  140.1 31.1 %all_to_all.40 = f32[16,64,256]{2,1,0:T(8,128)S(1)} all-to-all(f32[16,64,256]{2,1,0:T(8,128)S(1)} %copy.24), channel_id=1, replica_groups=mesh['blk'=16,'rep'=2] {'blk'}, dimensions={0} | all-to-all | bytes 2097152 | tf_op jit(solution)/shard_map/all_to_all | solution.py:79
  171.4 1.6 fusion.10
  (21 shorter events, 2.9 us)
Async XLA Ops:
  2.0 15.5 %all-to-all-start.2 = ((bf16[16,1,64]{2,1,0:T(2,128)(2,1)}), bf16[16,1,64]{2,1,0:T(2,128)(2,1)S(1)}, u32[]{:S(2)}, u32[]{:S(2)}) async-start(bf16[16,1,64]{2,1,0:T(2,128)(2,1)} %all_to_all.32), calls=%async_computation.2 | async-start | bytes 16384 | tf_op jit(solution)/shard_map/all_to_all | solution.py:31
  17.5 17.6 %all-to-all-start = ((bf16[16,64,256]{2,1,0:T(8,128)(2,1)}), bf16[16,64,256]{2,1,0:T(8,128)(2,1)S(1)}, u32[]{:S(2)}, u32[]{:S(2)}) async-start(bf16[16,64,256]{2,1,0:T(8,128)(2,1)} %bitcast.6), calls=%async_computation | async-start | bytes 1048576 | tf_op jit(solution)/shard_map/all_to_all | solution.py:30
  35.1 9.9 %all-to-all-start.3 = ((bf16[32,1,64]{2,1,0:T(2,128)(2,1)}), bf16[32,1,64]{2,1,0:T(2,128)(2,1)S(1)}, u32[]{:S(2)}, u32[]{:S(2)}) async-start(bf16[32,1,64]{2,1,0:T(2,128)(2,1)} %copy.20), calls=%async_computation.3 | async-start | bytes 32768 | tf_op jit(solution)/shard_map/all_to_all | solution.py:40
  45.0 28.9 %all-to-all-start.1 = ((bf16[32,64,256]{2,1,0:T(8,128)(2,1)}), bf16[32,64,256]{2,1,0:T(8,128)(2,1)S(1)}, u32[]{:S(2)}, u32[]{:S(2)}) async-start(bf16[32,64,256]{2,1,0:T(8,128)(2,1)} %broadcast_select_fusion), calls=%async_computation.1 | async-start | bytes 2097152 | tf_op jit(solution)/shard_map/all_to_all | solution.py:39
  139.5 31.9 %copy-start = (f32[1,1024,256]{2,1,0:T(8,128)S(1)}, f32[1,1024,256]{2,1,0:T(8,128)}, u32[]{:S(2)}) copy-start(f32[1,1024,256]{2,1,0:T(8,128)} %param.9) | copy-start | bytes 3145732
  139.5 31.9 %copy-start.1 = (f32[1,1024,256]{2,1,0:T(8,128)S(1)}, f32[1,1024,256]{2,1,0:T(8,128)}, u32[]{:S(2)}) copy-start(f32[1,1024,256]{2,1,0:T(8,128)} %param.10) | copy-start | bytes 3145732
where the time goes:
time: 174 us; the launch traced here: 173 us
  blocking collectives  83.1 us (48%)
  waiting for transfers between devices  47 us (27%)
  starting transfers between devices  17.3 us (10%)
  matrix products  10.4 us (6%)
  other arithmetic  7.47 us (4%)
  local copies, waits for them, and re-layouts  6.87 us (4%)
    all_to_all x1, blocking collectives, per_device(): lax.all_to_all(partials.reshape(requests, piece_rows, embed_width), ('blk...  52.1 us
    all_to_all x1, blocking collectives, per_device(): lax.all_to_all(summed.reshape(owners, piece_rows, embed_width), 'blk', sp...  31.1 us
    all_to_all x1, waiting for transfers between devices, per_device(): lax.all_to_all(outgoing, ('blk', 'rep'), split_axis=0, concat_axis=0, til...  26 us
    all_to_all x1, waiting for transfers between devices, per_device(): lax.all_to_all(own_vectors, 'blk', split_axis=0, concat_axis=0, tiled=True)  11.2 us
    all_to_all x1, starting transfers between devices, per_device(): lax.all_to_all(own_offsets, 'blk', split_axis=0, concat_axis=0, tiled=True)  8.31 us
    dot_general x1, matrix products, per_device(): lax.dot_general(row_vectors, col_vectors, (((1,), (1,)), ((), ())), prefe...  5.38 us
    all_to_all x1, waiting for transfers between devices, per_device(): lax.all_to_all(outgoing_offsets, ('blk', 'rep'), split_axis=0, concat_axi...  5.32 us
    all_to_all x1, waiting for transfers between devices, per_device(): lax.all_to_all(own_offsets, 'blk', split_axis=0, concat_axis=0, tiled=True)  4.43 us
  transfers between devices with their start and end apart: 4, of which 4 were waited for; matrix products, arithmetic and copies ran while one was open for 4% of the time, Pallas kernels for 0%

commit v1 on v0

v1 whole, which is shorter than its diff:
```python
import jax
import jax.numpy as jnp
from jax import lax
from jax.experimental import pallas as pl
from jax.experimental.pallas import tpu as pltpu
from jax.sharding import PartitionSpec as P

learn_rate = 0.05
conf_base = 0.1
conf_scale = 0.25

LANES = 128
ROWS = 256
VMEM_LIMIT = 32 * 1024 * 1024


def pow7(v):
    v2 = v * v
    return v2 * v2 * (v2 * v)


def pow5(v):
    v2 = v * v
    return v2 * v2 * v


def root(x, power):
    x = x.astype(jnp.float32)
    size = jnp.abs(x)
    r = jnp.exp(jnp.log(jnp.maximum(size, 1e-37)) * (1.0 / power))
    r = jnp.where(x < 0, -r, r)
    return jnp.where(size < 1e-37, 0.0, r)


def params():
    return pltpu.CompilerParams(vmem_limit_bytes=VMEM_LIMIT)


def pack_kernel(embed_ref, margin_ref, out_ref, spread):
    owners, message, _ = out_ref.shape
    rows = embed_ref.shape[0] // owners
    halves = embed_ref.shape[1] // LANES
    margin_rows = margin_ref.shape[1] // LANES
    for r in range(margin_rows):
        spread[r : r + 1, :] = margin_ref[0:1, r * LANES : (r + 1) * LANES].astype(jnp.float32)
    offsets = spread[...].astype(jnp.bfloat16)
    for s in range(owners):
        for h in range(halves):
            out_ref[s, h * rows : (h + 1) * rows, :] = embed_ref[
                s * rows : (s + 1) * rows, h * LANES : (h + 1) * LANES
            ].astype(jnp.bfloat16)
        out_ref[s, halves * rows :, :] = offsets


def pick_kernel(slot_ref, held_ref, out_ref, offsets_ref):
    requests, piece, _ = out_ref.shape
    offsets_ref[...] = held_ref[:, piece:, :]
    for r in range(requests):
        out_ref[r] = held_ref[slot_ref[r], :piece, :]


def tile_kernel(place_ref, counts_ref, arrived_ref, mine_ref, other_ref, out_ref, rows_v, cols_v, row_off, col_off, col_sum):
    step = pl.program_id(0)
    owners, _, piece, _ = arrived_ref.shape
    width = cols_v.shape[1]
    halves = width // LANES
    rows = piece // halves
    block = cols_v.shape[0]
    margin_rows = block // LANES

    @pl.when(step == 0)
    def _():
        for p in range(owners):
            for h in range(halves):
                rows_v[p * rows : (p + 1) * rows, h * LANES : (h + 1) * LANES] = arrived_ref[
                    p, 0, h * rows : (h + 1) * rows, :
                ]
                cols_v[p * rows : (p + 1) * rows, h * LANES : (h + 1) * LANES] = arrived_ref[
                    p, 1, h * rows : (h + 1) * rows, :
                ]
        plane = place_ref[0]
        row_slot = place_ref[1]
        col_slot = place_ref[2]
        row_m = jnp.where(plane == 0, mine_ref[row_slot], other_ref[row_slot]).astype(jnp.float32)
        col_m = jnp.where(plane == 0, other_ref[col_slot], mine_ref[col_slot]).astype(jnp.float32)
        turned = jnp.transpose(row_m)
        for r in range(margin_rows):
            row_off[r * LANES : (r + 1) * LANES, :] = turned[:, r : r + 1]
            col_off[:, r * LANES : (r + 1) * LANES] = col_m[r : r + 1, :]
        col_sum[...] = jnp.zeros_like(col_sum)

    here = pl.ds(pl.multiple_of(step * ROWS, ROWS), ROWS)
    row_vectors = rows_v[here, :]
    cols = cols_v[...]
    scores = lax.dot_general(
        row_vectors, cols, (((1,), (1,)), ((), ())), preferred_element_type=jnp.float32
    )
    tile_counts = counts_ref[0]
    present = tile_counts > 0
    counted = jnp.maximum(tile_counts, 1).astype(jnp.float32)
    shifted = scores + (row_off[here, :] + col_off[...])
    fitted = (conf_base + conf_scale * jnp.sqrt(counted)) * (shifted - jnp.log(counted))
    hinge = 1.0 / (1.0 + jnp.exp(-shifted))
    cell_grad = jnp.where(present, fitted, hinge).astype(jnp.bfloat16)
    row_gradient = pow7(jnp.dot(cell_grad, cols, preferred_element_type=jnp.float32)).astype(
        jnp.bfloat16
    )
    pieces = ROWS // rows
    for q in range(pieces):
        for h in range(halves):
            out_ref[step * pieces + q, 0, h * rows : (h + 1) * rows, :] = row_gradient[
                q * rows : (q + 1) * rows, h * LANES : (h + 1) * LANES
            ]
    col_sum[...] += lax.dot_general(
        cell_grad, row_vectors, (((0,), (0,)), ((), ())), preferred_element_type=jnp.float32
    )

    @pl.when(step == pl.num_programs(0) - 1)
    def _():
        for p in range(owners):
            for h in range(halves):
                out_ref[p, 1, h * rows : (h + 1) * rows, :] = pow7(
                    col_sum[p * rows : (p + 1) * rows, h * LANES : (h + 1) * LANES]
                ).astype(jnp.bfloat16)


def sum_kernel(slot_ref, returned_ref, out_ref, total):
    total[...] = jnp.zeros_like(total)
    for r in range(returned_ref.shape[0]):
        total[slot_ref[r]] += root(returned_ref[r], 7)
    for s in range(out_ref.shape[0]):
        out_ref[s] = pow5(total[s]).astype(jnp.bfloat16)


def update_kernel(sums_ref, embed_ref, accum_ref, new_embed_ref, new_accum_ref):
    pieces, piece, _ = sums_ref.shape
    halves = embed_ref.shape[1] // LANES
    rows = piece // halves
    for p in range(pieces):
        for h in range(halves):
            at = (slice(p * rows, (p + 1) * rows), slice(h * LANES, (h + 1) * LANES))
            gradient = root(sums_ref[p, h * rows : (h + 1) * rows, :], 5)
            new_accum = accum_ref[at] + gradient * gradient
            new_accum_ref[at] = new_accum
            new_embed_ref[at] = embed_ref[at] - learn_rate * gradient / jnp.sqrt(new_accum)


def per_device(counts, tile_list, owner_map, embed, accum, margins):
    owners = lax.axis_size("blk")
    requests = owners * lax.axis_size("rep")
    plane = lax.axis_index("rep")
    block, width = embed.shape[1:]
    piece = (block // owners) * (width // LANES)
    margin_rows = block // LANES
    smem = pl.BlockSpec(memory_space=pltpu.SMEM)
    f32, bf16 = jnp.float32, jnp.bfloat16

    wanted = jnp.stack([owner_map[k][tile_list[:, k]] for k in range(2)])
    slot_of = wanted[plane]
    me = lax.axis_index("blk") * lax.axis_size("rep") + plane
    place = jnp.concatenate([plane[None], wanted[:, me]]).astype(jnp.int32)

    outgoing = pl.pallas_call(
        pack_kernel,
        out_shape=jax.ShapeDtypeStruct((owners, piece + margin_rows, LANES), bf16),
        scratch_shapes=[pltpu.VMEM((margin_rows, LANES), f32)],
        compiler_params=params(),
        name="pack",
    )(embed[0], margins)
    held = lax.all_to_all(outgoing, "blk", split_axis=0, concat_axis=0, tiled=True)
    picked, offsets = pl.pallas_call(
        pick_kernel,
        in_specs=[smem, pl.BlockSpec(memory_space=pltpu.VMEM)],
        out_shape=(
            jax.ShapeDtypeStruct((requests, piece, LANES), bf16),
            jax.ShapeDtypeStruct((owners, margin_rows, LANES), bf16),
        ),
        compiler_params=params(),
        name="pick",
    )(slot_of, held)
    other_offsets = lax.ppermute(offsets, "rep", [(0, 1), (1, 0)])
    arrived = lax.all_to_all(picked, ("blk", "rep"), split_axis=0, concat_axis=0, tiled=True)
    whole = lambda *shape: pl.BlockSpec(shape, lambda i: (0,) * len(shape))
    partials = pl.pallas_call(
        tile_kernel,
        grid=(block // ROWS,),
        in_specs=[
            smem,
            pl.BlockSpec((1, ROWS, block), lambda i: (0, i, 0)),
            whole(owners, 2, piece, LANES),
            whole(owners, margin_rows, LANES),
            whole(owners, margin_rows, LANES),
        ],
        out_specs=whole(owners, 2, piece, LANES),
        out_shape=jax.ShapeDtypeStruct((owners, 2, piece, LANES), bf16),
        scratch_shapes=[
            pltpu.VMEM((block, width), bf16),
            pltpu.VMEM((block, width), bf16),
            pltpu.VMEM((block, 1), f32),
            pltpu.VMEM((1, block), f32),
            pltpu.VMEM((block, width), f32),
        ],
        compiler_params=params(),
        name="tile",
    )(place, counts, arrived.reshape(owners, 2, piece, LANES), offsets, other_offsets)
    returned = lax.all_to_all(
        partials.reshape(requests, piece, LANES), ("blk", "rep"), split_axis=0, concat_axis=0, tiled=True
    )
    sums = pl.pallas_call(
        sum_kernel,
        in_specs=[smem, pl.BlockSpec(memory_space=pltpu.VMEM)],
        out_shape=jax.ShapeDtypeStruct((owners, piece, LANES), bf16),
        scratch_shapes=[pltpu.VMEM((owners, piece, LANES), f32)],
        compiler_params=params(),
        name="sum",
    )(slot_of, returned)
    gradient = lax.all_to_all(sums, "blk", split_axis=0, concat_axis=0, tiled=True)
    new_embed, new_accum = pl.pallas_call(
        update_kernel,
        out_shape=(jax.ShapeDtypeStruct((block, width), f32),) * 2,
        compiler_params=params(),
        name="update",
    )(gradient, embed[0], accum[0])
    return (new_embed[None], new_accum[None])


def solution(mesh):
    in_specs = (
        P(("blk", "rep"), None, None),
        P(),
        P(),
        P("rep", "blk", None),
        P("rep", "blk", None),
        P("rep", "blk"),
    )
    out_specs = (P("rep", "blk", None), P("rep", "blk", None))
    return jax.shard_map(
        per_device, mesh=mesh, in_specs=in_specs, out_specs=out_specs, check_vma=False
    )
```

time: 174 us -> 121 us (0.70)
  blocking collectives: 83.1 us -> 49.4 us
  Pallas kernels: 0 us -> 13 us
  matrix products: 10.4 us -> 0 us
  waiting for transfers between devices: 47 us -> 38.4 us
  other arithmetic: 7.47 us -> 0.85 us
  starting transfers between devices: 17.3 us -> 11.6 us
    all_to_all x2, blocking collectives: 83.1 us -> 49.4 us  [the longest x1 29.7 us: per_device(): lax.all_to_all(partials.reshape(requests, piece, LANES), ('blk', 'rep'),...]
    pallas_call x0 -> x5, Pallas kernels: none -> 13 us  [the longest x1 6.67 us: per_device(): pl.pallas_call(tile_kernel, grid=(block // ROWS,), in_specs=[smem, pl.Blo...]
    dot_general x4 -> x0, matrix products: 10.4 us -> none  [the longest x1 5.38 us: per_device(): lax.dot_general(row_vectors, col_vectors, (((1,), (1,)), ((), ())), prefe...]
    all_to_all x4 -> x2, waiting for transfers between devices: 47 us -> 37.5 us  [the longest x1 24.8 us: per_device(): lax.all_to_all(picked, ('blk', 'rep'), split_axis=0, concat_axis=0, tiled...]
    all_to_all x4 -> x2, starting transfers between devices: 17.3 us -> 11.3 us  [the longest x1 8.31 us: per_device(): lax.all_to_all(outgoing, 'blk', split_axis=0, concat_axis=0, tiled=True)]
    unnamed x6 -> x10, local copies, waits for them, and re-layouts: 0.02 us -> 4.1 us
    dot_general x2 -> x0, local copies, waits for them, and re-layouts: 3.2 us -> none  [the longest x1 2.58 us: per_device(): lax.dot_general(cell_grad, row_vectors, (((0,), (0,)), ((), ())), preferr...]
    convert_element_type x2 -> x0, other arithmetic: 2.12 us -> none  [the longest x1 2.07 us: per_device(): embed[0].astype(jnp.bfloat16).reshape(owners, piece_rows, embed_width)]
  transfers between devices with their start and end apart: 4 -> 3, of which waited for: 4 -> 3; matrix products, arithmetic and copies ran while one was open for 4% -> 3% of each run, Pallas kernels for 0% -> 0%
where the time goes in v1:
time: 121 us
  blocking collectives  49.4 us (41%)
  waiting for transfers between devices  38.4 us (32%)
  Pallas kernels  13 us (11%)
  starting transfers between devices  11.6 us (10%)
  local copies, waits for them, and re-layouts  6.46 us (5%)
    all_to_all x1, blocking collectives, per_device(): lax.all_to_all(partials.reshape(requests, piece, LANES), ('blk', 'rep'),...  29.7 us
    all_to_all x1, waiting for transfers between devices, per_device(): lax.all_to_all(picked, ('blk', 'rep'), split_axis=0, concat_axis=0, tiled...  24.8 us
    all_to_all x1, blocking collectives, per_device(): lax.all_to_all(sums, 'blk', split_axis=0, concat_axis=0, tiled=True)  19.8 us
    all_to_all x1, waiting for transfers between devices, per_device(): lax.all_to_all(outgoing, 'blk', split_axis=0, concat_axis=0, tiled=True)  12.7 us
    all_to_all x1, starting transfers between devices, per_device(): lax.all_to_all(outgoing, 'blk', split_axis=0, concat_axis=0, tiled=True)  8.31 us
    pallas_call x1, Pallas kernels, per_device(): pl.pallas_call(tile_kernel, grid=(block // ROWS,), in_specs=[smem, pl.Blo...  6.67 us
    unnamed x10, local copies, waits for them, and re-layouts  4.1 us
    all_to_all x1, starting transfers between devices, per_device(): lax.all_to_all(picked, ('blk', 'rep'), split_axis=0, concat_axis=0, tiled...  3.01 us
  transfers between devices with their start and end apart: 3, of which 3 were waited for; matrix products, arithmetic and copies ran while one was open for 3% of the time, Pallas kernels for 0%

profile of v1, /device:TPU:0, one launch (start us, length us, event | category | flops | bytes accessed | tf_op | source)
XLA Modules:
  0.0 120.5 jit_solution(6052864934661503419)
XLA Ops:
  0.6 0.0 copy-start.1
  0.6 1.2 %copy-done.1 = f32[1,1024,256]{2,1,0:T(8,128)S(1)} copy-done((f32[1,1024,256]{2,1,0:T(8,128)S(1)}, f32[1,1024,256]{2,1,0:T(8,128)}, u32[]{:S(2)}) %copy-start.1) | copy-done | bytes 1048600
  1.9 0.7 copy-done.4
  2.5 0.9 pack.1
  3.4 8.3 %all-to-all-start = ((bf16[16,136,128]{2,1,0:T(8,128)(2,1)}), bf16[16,136,128]{2,1,0:T(8,128)(2,1)S(1)}, u32[]{:S(2)}, u32[]{:S(2)}) async-start(bf16[16,136,128]{2,1,0:T(8,128)(2,1)} %pack.1), calls=%async_computation | async-start | bytes 1114112 | tf_op jit(solution)/shard_map/all_to_all | solution.py:170
  11.7 0.8 fusion
  12.5 0.8 slice_bitcast_fusion.1
  13.3 0.7 gather_fusion.1
  14.0 0.7 gather_fusion
  14.7 12.7 %all-to-all-done.held_ref = bf16[16,136,128]{2,1,0:T(8,128)(2,1)S(1)} async-done(((bf16[16,136,128]{2,1,0:T(8,128)(2,1)}), bf16[16,136,128]{2,1,0:T(8,128)(2,1)S(1)}, u32[]{:S(2)}, u32[]{:S(2)}) %all-to-all-start) | async-done | bytes 557088 | tf_op jit(solution)/shard_map/all_to_all | solution.py:170
  27.4 1.6 %pick.1 = (bf16[32,128,128]{2,1,0:T(8,128)(2,1)}, bf16[16,8,128]{2,1,0:T(8,128)(2,1)S(1)}) custom-call(s32[32]{0:T(128)S(1)} %dynamic-slice_bitcast_fusion.slot_ref, bf16[16,136,128]{2,1,0:T(8,128)(2,1)S(1)} %all-to-all-done.held_ref), custom_call_target="tpu_custom_call" | custom-call | tf_op jit(solution)/shard_map/pick/pallas_call | solution.py:171
  29.0 3.0 %all-to-all-start.1 = ((bf16[32,128,128]{2,1,0:T(8,128)(2,1)}), bf16[32,128,128]{2,1,0:T(8,128)(2,1)S(1)}, u32[]{:S(2)}, u32[]{:S(2)}) async-start(bf16[32,128,128]{2,1,0:T(8,128)(2,1)} %get-tuple-element.6), calls=%async_computation.1 | async-start | bytes 2097152 | tf_op jit(solution)/shard_map/all_to_all | solution.py:182
  32.0 0.2 dynamic-slice_reduce_fusion
  32.2 0.3 collective-permute-start
  32.5 0.1 pad_add_fusion.1.place_ref
  32.6 0.9 collective-permute-done.other_ref
  33.5 24.8 %all-to-all-done.1 = bf16[32,128,128]{2,1,0:T(8,128)(2,1)S(1)} async-done(((bf16[32,128,128]{2,1,0:T(8,128)(2,1)}), bf16[32,128,128]{2,1,0:T(8,128)(2,1)S(1)}, u32[]{:S(2)}, u32[]{:S(2)}) %all-to-all-start.1) | async-done | bytes 1048608 | tf_op jit(solution)/shard_map/all_to_all | solution.py:182
  58.3 2.2 %copy-done = s32[1,1024,1024]{2,1,0:T(8,128)S(1)} copy-done((s32[1,1024,1024]{2,1,0:T(8,128)S(1)}, s32[1,1024,1024]{2,1,0:T(8,128)}, u32[]{:S(2)}) %copy-start) | copy-done | bytes 4194328
  60.5 6.7 %tile.1 = bf16[16,2,128,128]{3,2,1,0:T(8,128)(2,1)S(1)} custom-call(s32[3]{0:T(128)S(1)} %pad_add_fusion.1.place_ref, s32[1,1024,1024]{2,1,0:T(8,128)S(1)} %copy-done, bf16[16,2,128,128]{3,2,1,0:T(8,128)(2,1)S(1)} %bitcast.19, bf16[16,8,128]{2,1,0:T(8,128)(2,1)S(1)} %get-tuple-element.7.mine_ref, bf16[16,8,128]{2,1,0:T(8,128)(2,1)S(1)} %collective-permute-done.other_ref), custom_call_target="tpu_custom_call" | custom-call | tf_op jit(solution)/shard_map/tile/pallas_call | solution.py:184
  67.1 29.7 %all_to_all.20.returned_ref = bf16[32,128,128]{2,1,0:T(8,128)(2,1)S(1)} all-to-all(bf16[32,128,128]{2,1,0:T(8,128)(2,1)S(1)} %bitcast.20), channel_id=1, replica_groups=mesh['blk'=16,'rep'=2] {'blk','rep'}, dimensions={0} | all-to-all | bytes 2097152 | tf_op jit(solution)/shard_map/all_to_all | solution.py:206
  96.8 1.7 %sum.1 = bf16[16,128,128]{2,1,0:T(8,128)(2,1)S(1)} custom-call(s32[32]{0:T(128)S(1)} %dynamic-slice_bitcast_fusion.slot_ref, bf16[32,128,128]{2,1,0:T(8,128)(2,1)S(1)} %all_to_all.20.returned_ref), custom_call_target="tpu_custom_call" | custom-call | tf_op jit(solution)/shard_map/sum/pallas_call | solution.py:209
  98.5 19.8 %all_to_all.21.sums_ref = bf16[16,128,128]{2,1,0:T(8,128)(2,1)S(1)} all-to-all(bf16[16,128,128]{2,1,0:T(8,128)(2,1)S(1)} %sum.1), channel_id=1, replica_groups=mesh['blk'=16,'rep'=2] {'blk'}, dimensions={0} | all-to-all | bytes 1048576 | tf_op jit(solution)/shard_map/all_to_all | solution.py:217
  118.3 0.0 copy-done.3
  118.3 2.2 %update.1 = (f32[1024,256]{1,0:T(8,128)}, f32[1024,256]{1,0:T(8,128)}) custom-call(bf16[16,128,128]{2,1,0:T(8,128)(2,1)S(1)} %all_to_all.21.sums_ref, f32[1024,256]{1,0:T(8,128)S(1)} %bitcast.22, f32[1024,256]{1,0:T(8,128)S(1)} %bitcast.23), custom_call_target="tpu_custom_call" | custom-call | tf_op jit(solution)/shard_map/update/pallas_call | solution.py:218
  (8 shorter events, 0.0 us)
Async XLA Ops:
  0.6 1.2 %copy-start.1 = (f32[1,1024,256]{2,1,0:T(8,128)S(1)}, f32[1,1024,256]{2,1,0:T(8,128)}, u32[]{:S(2)}) copy-start(f32[1,1024,256]{2,1,0:T(8,128)} %param.9) | copy-start | bytes 3145732
  1.9 0.7 copy-start.4
  3.4 24.0 %all-to-all-start = ((bf16[16,136,128]{2,1,0:T(8,128)(2,1)}), bf16[16,136,128]{2,1,0:T(8,128)(2,1)S(1)}, u32[]{:S(2)}, u32[]{:S(2)}) async-start(bf16[16,136,128]{2,1,0:T(8,128)(2,1)} %pack.1), calls=%async_computation | async-start | bytes 1114112 | tf_op jit(solution)/shard_map/all_to_all | solution.py:170
  29.0 29.3 %all-to-all-start.1 = ((bf16[32,128,128]{2,1,0:T(8,128)(2,1)}), bf16[32,128,128]{2,1,0:T(8,128)(2,1)S(1)}, u32[]{:S(2)}, u32[]{:S(2)}) async-start(bf16[32,128,128]{2,1,0:T(8,128)(2,1)} %get-tuple-element.6), calls=%async_computation.1 | async-start | bytes 2097152 | tf_op jit(solution)/shard_map/all_to_all | solution.py:182
  32.2 1.3 %collective-permute-start = (bf16[16,8,128]{2,1,0:T(8,128)(2,1)S(1)}, bf16[16,8,128]{2,1,0:T(8,128)(2,1)S(1)}, u32[]{:S(2)}, u32[]{:S(2)}) collective-permute-start(bf16[16,8,128]{2,1,0:T(8,128)(2,1)S(1)} %get-tuple-element.7.mine_ref), channel_id=1, source_target_pairs={{0,1},{1,0},{2,3},{3,2},{4,5},{5,4},{6,7},{7,6},{8,9},{9,8},{10,11... | collective-permute-start | bytes 98312 | tf_op jit(solution)/shard_map/ppermute | solution.py:181
  58.3 2.2 %copy-start = (s32[1,1024,1024]{2,1,0:T(8,128)S(1)}, s32[1,1024,1024]{2,1,0:T(8,128)}, u32[]{:S(2)}) copy-start(s32[1,1024,1024]{2,1,0:T(8,128)} %counts_ref.1) | copy-start | bytes 12582916
  60.5 57.8 %copy-start.2 = (f32[1,1024,256]{2,1,0:T(8,128)S(1)}, f32[1,1024,256]{2,1,0:T(8,128)}, u32[]{:S(2)}) copy-start(f32[1,1024,256]{2,1,0:T(8,128)} %param.9) | copy-start | bytes 3145732
  60.5 57.8 %copy-start.3 = (f32[1,1024,256]{2,1,0:T(8,128)S(1)}, f32[1,1024,256]{2,1,0:T(8,128)}, u32[]{:S(2)}) copy-start(f32[1,1024,256]{2,1,0:T(8,128)} %param.10) | copy-start | bytes 3145732

commit v2 on v1

v2 whole, which is shorter than its diff:
```python
import jax
import jax.numpy as jnp
from jax import lax
from jax.experimental import pallas as pl
from jax.experimental.pallas import tpu as pltpu
from jax.sharding import PartitionSpec as P

learn_rate = 0.05
conf_base = 0.1
conf_scale = 0.25

LANES = 128
ROWS = 256
MIB = 1024 * 1024


def code(v):
    return (v * v) * (v * jnp.abs(v))


def decode(x):
    x = x.astype(jnp.float32)
    size = jnp.maximum(jnp.abs(x), 1e-37)
    once = lax.rsqrt(size)
    return (x * once) * lax.rsqrt(size * once)


def params(mib):
    return pltpu.CompilerParams(vmem_limit_bytes=mib * MIB)


def pack_kernel(embed_ref, margin_ref, out_ref, spread):
    pieces, message, _ = out_ref.shape
    rows = embed_ref.shape[0] // pieces
    halves = embed_ref.shape[1] // LANES
    margin_rows = margin_ref.shape[1] // LANES
    for r in range(margin_rows):
        spread[r : r + 1, :] = margin_ref[0:1, r * LANES : (r + 1) * LANES].astype(jnp.float32)
    offsets = spread[...].astype(jnp.bfloat16)
    for s in range(pieces):
        for h in range(halves):
            out_ref[s, h * rows : (h + 1) * rows, :] = embed_ref[
                s * rows : (s + 1) * rows, h * LANES : (h + 1) * LANES
            ].astype(jnp.bfloat16)
        out_ref[s, halves * rows :, :] = offsets


def pick_kernel(slot_ref, held_ref, out_ref, offsets_ref):
    requests, rows, width = out_ref.shape
    halves = width // LANES
    offsets_ref[...] = held_ref[:, rows * halves :, :]
    for r in range(requests):
        for h in range(halves):
            out_ref[r, :, h * LANES : (h + 1) * LANES] = held_ref[
                slot_ref[r], h * rows : (h + 1) * rows, :
            ]


def tile_kernel(
    place_ref, counts_ref, arrived_ref, mine_ref, other_ref, out_ref, counts_v, row_off, col_off, copied
):
    owners, _, rows, width = arrived_ref.shape
    block = counts_v.shape[0]
    steps = block // ROWS
    copies = []
    for step in range(steps):
        here = pl.ds(step * ROWS, ROWS)
        copies.append(
            pltpu.make_async_copy(counts_ref.at[0, here, :], counts_v.at[here, :], copied.at[step])
        )
        copies[-1].start()
    plane = place_ref[0]
    row_slot = place_ref[1]
    col_slot = place_ref[2]
    row_m = jnp.where(plane == 0, mine_ref[row_slot], other_ref[row_slot]).astype(jnp.float32)
    col_m = jnp.where(plane == 0, other_ref[col_slot], mine_ref[col_slot]).astype(jnp.float32)
    turned = jnp.transpose(row_m)
    for r in range(block // LANES):
        row_off[r * LANES : (r + 1) * LANES, :] = turned[:, r : r + 1]
        col_off[:, r * LANES : (r + 1) * LANES] = col_m[r : r + 1, :]
    cols = arrived_ref[:, 1].reshape(block, width)
    pieces = ROWS // rows
    col_sum = None
    for step in range(steps):
        here = slice(step * ROWS, (step + 1) * ROWS)
        there = slice(step * pieces, (step + 1) * pieces)
        row_vectors = arrived_ref[there, 0].reshape(ROWS, width)
        scores = lax.dot_general(
            row_vectors, cols, (((1,), (1,)), ((), ())), preferred_element_type=jnp.float32
        )
        shifted = scores + (row_off[here, :] + col_off[...])
        copies[step].wait()
        tile_counts = counts_v[here, :].astype(jnp.float32)
        counted = jnp.maximum(tile_counts, 1.0)
        confidence = conf_base + conf_scale * (counted * lax.rsqrt(counted))
        fitted = confidence * (shifted - jnp.log(counted))
        hinge = 0.5 + 0.5 * jnp.tanh(0.5 * shifted)
        cell_grad = jnp.where(tile_counts > 0, fitted, hinge).astype(jnp.bfloat16)
        row_gradient = jnp.dot(cell_grad, cols, preferred_element_type=jnp.float32)
        out_ref[there, 0] = code(row_gradient).astype(jnp.bfloat16).reshape(pieces, rows, width)
        part = lax.dot_general(
            cell_grad, row_vectors, (((0,), (0,)), ((), ())), preferred_element_type=jnp.float32
        )
        col_sum = part if step == 0 else col_sum + part
    out_ref[:, 1] = code(col_sum).astype(jnp.bfloat16).reshape(owners, rows, width)


def sum_kernel(slot_ref, returned_ref, out_ref, total):
    total[...] = jnp.zeros_like(total)
    for r in range(returned_ref.shape[0]):
        total[slot_ref[r]] += decode(returned_ref[r])
    out_ref[...] = code(total[...]).astype(jnp.bfloat16)


def update_kernel(sums_ref, embed_ref, accum_ref, new_embed_ref, new_accum_ref):
    gradient = decode(sums_ref[...].reshape(embed_ref.shape))
    new_accum = accum_ref[...] + gradient * gradient
    new_accum_ref[...] = new_accum
    new_embed_ref[...] = embed_ref[...] - learn_rate * gradient * lax.rsqrt(new_accum)


def per_device(counts, tile_list, owner_map, embed, accum, margins):
    owners = lax.axis_size("blk")
    requests = owners * lax.axis_size("rep")
    plane = lax.axis_index("rep")
    block, width = embed.shape[1:]
    rows = block // owners
    halves = width // LANES
    margin_rows = block // LANES
    smem = pl.BlockSpec(memory_space=pltpu.SMEM)
    vmem = pl.BlockSpec(memory_space=pltpu.VMEM)
    f32, bf16 = jnp.float32, jnp.bfloat16

    wanted = jnp.stack([owner_map[k][tile_list[:, k]] for k in range(2)])
    slot_of = wanted[plane]
    me = lax.axis_index("blk") * lax.axis_size("rep") + plane
    place = jnp.concatenate([plane[None], wanted[:, me]]).astype(jnp.int32)

    steps = 2
    outgoing = pl.pallas_call(
        pack_kernel,
        grid=(steps,),
        in_specs=[
            pl.BlockSpec((block // steps, width), lambda i: (i, 0)),
            pl.BlockSpec((1, block), lambda i: (0, 0)),
        ],
        out_specs=pl.BlockSpec((owners // steps, halves * rows + margin_rows, LANES), lambda i: (i, 0, 0)),
        out_shape=jax.ShapeDtypeStruct((owners, halves * rows + margin_rows, LANES), bf16),
        scratch_shapes=[pltpu.VMEM((margin_rows, LANES), f32)],
        compiler_params=params(60),
        name="pack",
    )(embed[0], margins)
    held = lax.all_to_all(outgoing, "blk", split_axis=0, concat_axis=0, tiled=True)
    picked, offsets = pl.pallas_call(
        pick_kernel,
        in_specs=[smem, vmem],
        out_shape=(
            jax.ShapeDtypeStruct((requests, rows, width), bf16),
            jax.ShapeDtypeStruct((owners, margin_rows, LANES), bf16),
        ),
        compiler_params=params(16),
        name="pick",
    )(slot_of, held)
    other_offsets = lax.ppermute(offsets, "rep", [(0, 1), (1, 0)])
    arrived = lax.all_to_all(picked, ("blk", "rep"), split_axis=0, concat_axis=0, tiled=True)
    partials = pl.pallas_call(
        tile_kernel,
        in_specs=[smem, pl.BlockSpec(memory_space=pltpu.HBM)] + [vmem] * 3,
        out_shape=jax.ShapeDtypeStruct((owners, 2, rows, width), bf16),
        scratch_shapes=[
            pltpu.VMEM((block, block), jnp.int32),
            pltpu.VMEM((block, 1), f32),
            pltpu.VMEM((1, block), f32),
            pltpu.SemaphoreType.DMA((block // ROWS,)),
        ],
        compiler_params=params(24),
        name="tile",
    )(place, pltpu.with_memory_space_constraint(counts, pltpu.HBM), arrived.reshape(owners, 2, rows, width), offsets, other_offsets)
    returned = lax.all_to_all(
        partials.reshape(requests, rows, width), ("blk", "rep"), split_axis=0, concat_axis=0, tiled=True
    )
    sums = pl.pallas_call(
        sum_kernel,
        in_specs=[smem, vmem],
        out_shape=jax.ShapeDtypeStruct((owners, rows, width), bf16),
        scratch_shapes=[pltpu.VMEM((owners, rows, width), f32)],
        compiler_params=params(16),
        name="sum",
    )(slot_of, returned)
    gradient = lax.all_to_all(sums, "blk", split_axis=0, concat_axis=0, tiled=True)
    steps = 4
    part = pl.BlockSpec((block // steps, width), lambda i: (i, 0))
    new_embed, new_accum = pl.pallas_call(
        update_kernel,
        grid=(steps,),
        in_specs=[pl.BlockSpec((owners // steps, rows, width), lambda i: (i, 0, 0)), part, part],
        out_specs=(part, part),
        out_shape=(jax.ShapeDtypeStruct((block, width), f32),) * 2,
        compiler_params=params(16),
        name="update",
    )(gradient, embed[0], accum[0])
    return (new_embed[None], new_accum[None])


def solution(mesh):
    in_specs = (
        P(("blk", "rep"), None, None),
        P(),
        P(),
        P("rep", "blk", None),
        P("rep", "blk", None),
        P("rep", "blk"),
    )
    out_specs = (P("rep", "blk", None), P("rep", "blk", None))
    return jax.shard_map(
        per_device, mesh=mesh, in_specs=in_specs, out_specs=out_specs, check_vma=False
    )
```

time: 121 us -> 117 us (0.967)
  local copies, waits for them, and re-layouts: 6.46 us -> 2.36 us
    unnamed x10 -> x4, local copies, waits for them, and re-layouts: 4.1 us -> 0.01 us
where the time goes in v2:
time: 117 us; the launch traced here: 116 us
  blocking collectives  49.4 us (42%)
  waiting for transfers between devices  38.4 us (33%)
  Pallas kernels  12.9 us (11%)
  starting transfers between devices  11.6 us (10%)
  local copies, waits for them, and re-layouts  2.36 us (2%)
    all_to_all x1, blocking collectives, per_device(): lax.all_to_all(partials.reshape(requests, rows, width), ('blk', 'rep'), s...  29.7 us
    all_to_all x1, waiting for transfers between devices, per_device(): lax.all_to_all(picked, ('blk', 'rep'), split_axis=0, concat_axis=0, tiled...  24.8 us
    all_to_all x1, blocking collectives, per_device(): lax.all_to_all(sums, 'blk', split_axis=0, concat_axis=0, tiled=True)  19.8 us
    all_to_all x1, waiting for transfers between devices, per_device(): lax.all_to_all(outgoing, 'blk', split_axis=0, concat_axis=0, tiled=True)  12.7 us
    all_to_all x1, starting transfers between devices, per_device(): lax.all_to_all(outgoing, 'blk', split_axis=0, concat_axis=0, tiled=True)  8.31 us
    pallas_call x1, Pallas kernels, per_device(): pl.pallas_call(tile_kernel, in_specs=[smem, pl.BlockSpec(memory_space=plt...  5.48 us
    all_to_all x1, starting transfers between devices, per_device(): lax.all_to_all(picked, ('blk', 'rep'), split_axis=0, concat_axis=0, tiled...  3.01 us
  transfers between devices with their start and end apart: 3, of which 3 were waited for; matrix products, arithmetic and copies ran while one was open for 3% of the time, Pallas kernels for 0%

profile of v2, /device:TPU:0, one launch (start us, length us, event | category | flops | bytes accessed | tf_op | source)
XLA Modules:
  0.0 116.2 jit_solution(409757951326027083)
XLA Ops:
  0.6 2.0 %pack.1 = bf16[16,136,128]{2,1,0:T(8,128)(2,1)} custom-call(f32[1024,256]{1,0:T(8,128)} %bitcast.21, bf16[1,1024]{1,0:T(2,128)(2,1)} %margin_ref.1), custom_call_target="tpu_custom_call" | custom-call | tf_op jit(solution)/shard_map/pack/pallas_call | solution.py:140
  2.6 8.3 %all-to-all-start = ((bf16[16,136,128]{2,1,0:T(8,128)(2,1)}), bf16[16,136,128]{2,1,0:T(8,128)(2,1)S(1)}, u32[]{:S(2)}, u32[]{:S(2)}) async-start(bf16[16,136,128]{2,1,0:T(8,128)(2,1)} %pack.1), calls=%async_computation | async-start | bytes 1114112 | tf_op jit(solution)/shard_map/all_to_all | solution.py:153
  10.9 0.8 fusion
  11.7 0.8 slice_bitcast_fusion.1
  12.5 0.7 gather_fusion.1
  13.2 0.7 gather_fusion
  13.9 12.7 %all-to-all-done.held_ref = bf16[16,136,128]{2,1,0:T(8,128)(2,1)S(1)} async-done(((bf16[16,136,128]{2,1,0:T(8,128)(2,1)}), bf16[16,136,128]{2,1,0:T(8,128)(2,1)S(1)}, u32[]{:S(2)}, u32[]{:S(2)}) %all-to-all-start) | async-done | bytes 557088 | tf_op jit(solution)/shard_map/all_to_all | solution.py:153
  26.6 1.7 %pick.1 = (bf16[32,64,256]{2,1,0:T(8,128)(2,1)}, bf16[16,8,128]{2,1,0:T(8,128)(2,1)S(1)}) custom-call(s32[32]{0:T(128)S(1)} %dynamic-slice_bitcast_fusion.slot_ref, bf16[16,136,128]{2,1,0:T(8,128)(2,1)S(1)} %all-to-all-done.held_ref), custom_call_target="tpu_custom_call" | custom-call | tf_op jit(solution)/shard_map/pick/pallas_call | solution.py:154
  28.3 3.0 %all-to-all-start.1 = ((bf16[32,64,256]{2,1,0:T(8,128)(2,1)}), bf16[32,64,256]{2,1,0:T(8,128)(2,1)S(1)}, u32[]{:S(2)}, u32[]{:S(2)}) async-start(bf16[32,64,256]{2,1,0:T(8,128)(2,1)} %get-tuple-element.6), calls=%async_computation.1 | async-start | bytes 2097152 | tf_op jit(solution)/shard_map/all_to_all | solution.py:165
  31.4 0.2 dynamic-slice_reduce_fusion
  31.5 0.3 collective-permute-start
  31.9 0.1 pad_add_fusion.1.place_ref
  31.9 0.9 collective-permute-done.other_ref
  32.8 24.8 %all-to-all-done.1 = bf16[32,64,256]{2,1,0:T(8,128)(2,1)S(1)} async-done(((bf16[32,64,256]{2,1,0:T(8,128)(2,1)}), bf16[32,64,256]{2,1,0:T(8,128)(2,1)S(1)}, u32[]{:S(2)}, u32[]{:S(2)}) %all-to-all-start.1) | async-done | bytes 1048608 | tf_op jit(solution)/shard_map/all_to_all | solution.py:165
  57.6 0.0 copy-start
  57.6 0.0 copy-start.1
  57.6 5.5 %tile.1 = bf16[16,2,64,256]{3,2,1,0:T(8,128)(2,1)S(1)} custom-call(s32[3]{0:T(128)S(1)} %pad_add_fusion.1.place_ref, s32[1,1024,1024]{2,1,0:T(8,128)} %counts_ref.1, bf16[16,2,64,256]{3,2,1,0:T(8,128)(2,1)S(1)} %bitcast.19, bf16[16,8,128]{2,1,0:T(8,128)(2,1)S(1)} %get-tuple-element.7.mine_ref, bf16[16,8,128]{2,1,0:T(8,128)(2,1)S(1)} %collective-permute-done.other_ref), custom_call_target="tpu_custom_call" | custom-call | tf_op jit(solution)/shard_map/tile/pallas_call | solution.py:166
  63.1 29.7 %all_to_all.20.returned_ref = bf16[32,64,256]{2,1,0:T(8,128)(2,1)S(1)} all-to-all(bf16[32,64,256]{2,1,0:T(8,128)(2,1)S(1)} %bitcast.20), channel_id=1, replica_groups=mesh['blk'=16,'rep'=2] {'blk','rep'}, dimensions={0} | all-to-all | bytes 2097152 | tf_op jit(solution)/shard_map/all_to_all | solution.py:179
  92.8 1.7 %sum.1 = bf16[16,64,256]{2,1,0:T(8,128)(2,1)S(1)} custom-call(s32[32]{0:T(128)S(1)} %dynamic-slice_bitcast_fusion.slot_ref, bf16[32,64,256]{2,1,0:T(8,128)(2,1)S(1)} %all_to_all.20.returned_ref), custom_call_target="tpu_custom_call" | custom-call | tf_op jit(solution)/shard_map/sum/pallas_call | solution.py:182
  94.4 19.8 %all_to_all.21.sums_ref = bf16[16,64,256]{2,1,0:T(8,128)(2,1)S(1)} all-to-all(bf16[16,64,256]{2,1,0:T(8,128)(2,1)S(1)} %sum.1), channel_id=1, replica_groups=mesh['blk'=16,'rep'=2] {'blk'}, dimensions={0} | all-to-all | bytes 1048576 | tf_op jit(solution)/shard_map/all_to_all | solution.py:190
  114.2 0.0 copy-done
  114.2 0.0 copy-done.1
  114.2 2.0 %update.1 = (f32[1024,256]{1,0:T(8,128)}, f32[1024,256]{1,0:T(8,128)}) custom-call(bf16[16,64,256]{2,1,0:T(8,128)(2,1)S(1)} %all_to_all.21.sums_ref, f32[1024,256]{1,0:T(8,128)S(1)} %bitcast.22, f32[1024,256]{1,0:T(8,128)S(1)} %bitcast.23), custom_call_target="tpu_custom_call" | custom-call | tf_op jit(solution)/shard_map/update/pallas_call | solution.py:193
  (3 shorter events, 0.0 us)
Async XLA Ops:
  2.6 24.0 %all-to-all-start = ((bf16[16,136,128]{2,1,0:T(8,128)(2,1)}), bf16[16,136,128]{2,1,0:T(8,128)(2,1)S(1)}, u32[]{:S(2)}, u32[]{:S(2)}) async-start(bf16[16,136,128]{2,1,0:T(8,128)(2,1)} %pack.1), calls=%async_computation | async-start | bytes 1114112 | tf_op jit(solution)/shard_map/all_to_all | solution.py:153
  28.3 29.3 %all-to-all-start.1 = ((bf16[32,64,256]{2,1,0:T(8,128)(2,1)}), bf16[32,64,256]{2,1,0:T(8,128)(2,1)S(1)}, u32[]{:S(2)}, u32[]{:S(2)}) async-start(bf16[32,64,256]{2,1,0:T(8,128)(2,1)} %get-tuple-element.6), calls=%async_computation.1 | async-start | bytes 2097152 | tf_op jit(solution)/shard_map/all_to_all | solution.py:165
  31.5 1.3 %collective-permute-start = (bf16[16,8,128]{2,1,0:T(8,128)(2,1)S(1)}, bf16[16,8,128]{2,1,0:T(8,128)(2,1)S(1)}, u32[]{:S(2)}, u32[]{:S(2)}) collective-permute-start(bf16[16,8,128]{2,1,0:T(8,128)(2,1)S(1)} %get-tuple-element.7.mine_ref), channel_id=1, source_target_pairs={{0,1},{1,0},{2,3},{3,2},{4,5},{5,4},{6,7},{7,6},{8,9},{9,8},{10,11... | collective-permute-start | bytes 98312 | tf_op jit(solution)/shard_map/ppermute | solution.py:164
  57.6 56.6 %copy-start = (f32[1,1024,256]{2,1,0:T(8,128)S(1)}, f32[1,1024,256]{2,1,0:T(8,128)}, u32[]{:S(2)}) copy-start(f32[1,1024,256]{2,1,0:T(8,128)} %param.9) | copy-start | bytes 3145732
  57.6 56.6 %copy-start.1 = (f32[1,1024,256]{2,1,0:T(8,128)S(1)}, f32[1,1024,256]{2,1,0:T(8,128)}, u32[]{:S(2)}) copy-start(f32[1,1024,256]{2,1,0:T(8,128)} %param.10) | copy-start | bytes 3145732

commit v3 on v2

--- a/solution.py
+++ b/solution.py
@@ -45,30 +45,32 @@
         out_ref[s, halves * rows :, :] = offsets
 
 
-def pick_kernel(slot_ref, held_ref, out_ref, offsets_ref):
-    requests, rows, width = out_ref.shape
-    halves = width // LANES
-    offsets_ref[...] = held_ref[:, rows * halves :, :]
+def pick_kernel(slot_ref, held_ref, out_ref, offsets_ref, copied):
+    requests, piece, _ = out_ref.shape
+    copies = []
     for r in range(requests):
-        for h in range(halves):
-            out_ref[r, :, h * LANES : (h + 1) * LANES] = held_ref[
-                slot_ref[r], h * rows : (h + 1) * rows, :
-            ]
-
-
-def tile_kernel(
-    place_ref, counts_ref, arrived_ref, mine_ref, other_ref, out_ref, counts_v, row_off, col_off, copied
-):
-    owners, _, rows, width = arrived_ref.shape
-    block = counts_v.shape[0]
-    steps = block // ROWS
-    copies = []
-    for step in range(steps):
-        here = pl.ds(step * ROWS, ROWS)
         copies.append(
-            pltpu.make_async_copy(counts_ref.at[0, here, :], counts_v.at[here, :], copied.at[step])
+            pltpu.make_async_copy(
+                held_ref.at[slot_ref[r], pl.ds(0, piece), :], out_ref.at[r], copied.at[r]
+            )
         )
         copies[-1].start()
+    offsets_ref[...] = held_ref[:, piece:, :]
+    for copy in copies:
+        copy.wait()
+
+
+def tile_kernel(
+    place_ref, counts_ref, arrived_ref, mine_ref, other_ref, out_ref, row_off, col_off
+):
+    owners, _, rows, width = out_ref.shape
+    halves = width // LANES
+    block = counts_ref.shape[0]
+
+    def vectors(pieces, plane):
+        parts = [arrived_ref[pieces, plane, h * rows : (h + 1) * rows, :] for h in range(halves)]
+        return jnp.concatenate([p.reshape(-1, LANES) for p in parts], axis=1)
+
     plane = place_ref[0]
     row_slot = place_ref[1]
     col_slot = place_ref[2]
@@ -78,19 +80,18 @@
     for r in range(block // LANES):
         row_off[r * LANES : (r + 1) * LANES, :] = turned[:, r : r + 1]
         col_off[:, r * LANES : (r + 1) * LANES] = col_m[r : r + 1, :]
-    cols = arrived_ref[:, 1].reshape(block, width)
+    cols = vectors(slice(0, owners), 1)
     pieces = ROWS // rows
     col_sum = None
-    for step in range(steps):
+    for step in range(block // ROWS):
         here = slice(step * ROWS, (step + 1) * ROWS)
         there = slice(step * pieces, (step + 1) * pieces)
-        row_vectors = arrived_ref[there, 0].reshape(ROWS, width)
+        row_vectors = vectors(there, 0)
         scores = lax.dot_general(
             row_vectors, cols, (((1,), (1,)), ((), ())), preferred_element_type=jnp.float32
         )
         shifted = scores + (row_off[here, :] + col_off[...])
-        copies[step].wait()
-        tile_counts = counts_v[here, :].astype(jnp.float32)
+        tile_counts = counts_ref[here, :].astype(jnp.float32)
         counted = jnp.maximum(tile_counts, 1.0)
         confidence = conf_base + conf_scale * (counted * lax.rsqrt(counted))
         fitted = confidence * (shifted - jnp.log(counted))
@@ -112,11 +113,26 @@
     out_ref[...] = code(total[...]).astype(jnp.bfloat16)
 
 
-def update_kernel(sums_ref, embed_ref, accum_ref, new_embed_ref, new_accum_ref):
-    gradient = decode(sums_ref[...].reshape(embed_ref.shape))
-    new_accum = accum_ref[...] + gradient * gradient
-    new_accum_ref[...] = new_accum
-    new_embed_ref[...] = embed_ref[...] - learn_rate * gradient * lax.rsqrt(new_accum)
+def update_kernel(
+    sums_ref, embed_ref, accum_ref, new_embed_ref, new_accum_ref, embed_v, accum_v, copied
+):
+    pieces, rows, width = sums_ref.shape
+    steps = copied.shape[1]
+    copies = []
+    for step in range(steps):
+        some = pieces // steps
+        here = pl.ds(step * some * rows, some * rows)
+        gradient = decode(sums_ref[step * some : (step + 1) * some].reshape(some * rows, width))
+        new_accum = accum_ref[here, :] + gradient * gradient
+        accum_v[here, :] = new_accum
+        embed_v[here, :] = embed_ref[here, :] - learn_rate * gradient * lax.rsqrt(new_accum)
+        for k, (new_v, new_ref) in enumerate(((accum_v, new_accum_ref), (embed_v, new_embed_ref))):
+            copies.append(
+                pltpu.make_async_copy(new_v.at[here, :], new_ref.at[here, :], copied.at[k, step])
+            )
+            copies[-1].start()
+    for copy in copies:
+        copy.wait()
 
 
 def per_device(counts, tile_list, owner_map, embed, accum, margins):
@@ -154,10 +170,12 @@
     picked, offsets = pl.pallas_call(
         pick_kernel,
         in_specs=[smem, vmem],
+        out_specs=(pl.BlockSpec(memory_space=pl.ANY), vmem),
         out_shape=(
-            jax.ShapeDtypeStruct((requests, rows, width), bf16),
+            jax.ShapeDtypeStruct((requests, halves * rows, LANES), bf16),
             jax.ShapeDtypeStruct((owners, margin_rows, LANES), bf16),
         ),
+        scratch_shapes=[pltpu.SemaphoreType.DMA((requests,))],
         compiler_params=params(16),
         name="pick",
     )(slot_of, held)
@@ -165,17 +183,15 @@
     arrived = lax.all_to_all(picked, ("blk", "rep"), split_axis=0, concat_axis=0, tiled=True)
     partials = pl.pallas_call(
         tile_kernel,
-        in_specs=[smem, pl.BlockSpec(memory_space=pltpu.HBM)] + [vmem] * 3,
+        in_specs=[smem] + [vmem] * 4,
         out_shape=jax.ShapeDtypeStruct((owners, 2, rows, width), bf16),
         scratch_shapes=[
-            pltpu.VMEM((block, block), jnp.int32),
             pltpu.VMEM((block, 1), f32),
             pltpu.VMEM((1, block), f32),
-            pltpu.SemaphoreType.DMA((block // ROWS,)),
         ],
         compiler_params=params(24),
         name="tile",
-    )(place, pltpu.with_memory_space_constraint(counts, pltpu.HBM), arrived.reshape(owners, 2, rows, width), offsets, other_offsets)
+    )(place, counts[0].astype(bf16), arrived.reshape(owners, 2, halves * rows, LANES), offsets, other_offsets)
     returned = lax.all_to_all(
         partials.reshape(requests, rows, width), ("blk", "rep"), split_axis=0, concat_axis=0, tiled=True
     )
@@ -188,14 +204,16 @@
         name="sum",
     )(slot_of, returned)
     gradient = lax.all_to_all(sums, "blk", split_axis=0, concat_axis=0, tiled=True)
-    steps = 4
-    part = pl.BlockSpec((block // steps, width), lambda i: (i, 0))
     new_embed, new_accum = pl.pallas_call(
         update_kernel,
-        grid=(steps,),
-        in_specs=[pl.BlockSpec((owners // steps, rows, width), lambda i: (i, 0, 0)), part, part],
-        out_specs=(part, part),
+        in_specs=[vmem] * 3,
+        out_specs=(pl.BlockSpec(memory_space=pl.ANY),) * 2,
         out_shape=(jax.ShapeDtypeStruct((block, width), f32),) * 2,
+        scratch_shapes=[
+            pltpu.VMEM((block, width), f32),
+            pltpu.VMEM((block, width), f32),
+            pltpu.SemaphoreType.DMA((2, 4)),
+        ],
         compiler_params=params(16),
         name="update",
     )(gradient, embed[0], accum[0])

time: 117 us -> 115 us (0.983)
  waiting for transfers between devices: 38.4 us -> 35.6 us
  other arithmetic: 0.85 us -> 3.62 us
  Pallas kernels: 12.9 us -> 11.1 us
    all_to_all x1, waiting for transfers between devices: 24.8 us -> 22 us  [per_device(): lax.all_to_all(picked, ('blk', 'rep'), split_axis=0, concat_axis=0, tiled...]
    convert_element_type x0 -> x1, other arithmetic: none -> 2.76 us  [per_device(): counts[0].astype(bf16)]
    pallas_call x3, Pallas kernels: 9.23 us -> 7.47 us  [the longest x1 4.19 us: per_device(): pl.pallas_call(tile_kernel, in_specs=[smem] + [vmem] * 4, out_shape=jax.S...]
  transfers between devices with their start and end apart: 3 -> 3, of which waited for: 3 -> 3; matrix products, arithmetic and copies ran while one was open for 3% -> 5% of each run, Pallas kernels for 0% -> 0%
where the time goes in v3:
time: 115 us
  blocking collectives  49.4 us (43%)
  waiting for transfers between devices  35.6 us (31%)
  starting transfers between devices  11.6 us (10%)
  Pallas kernels  11.1 us (10%)
  other arithmetic  3.62 us (3%)
  local copies, waits for them, and re-layouts  2.36 us (2%)
    all_to_all x1, blocking collectives, per_device(): lax.all_to_all(partials.reshape(requests, rows, width), ('blk', 'rep'), s...  29.7 us
    all_to_all x1, waiting for transfers between devices, per_device(): lax.all_to_all(picked, ('blk', 'rep'), split_axis=0, concat_axis=0, tiled...  22 us
    all_to_all x1, blocking collectives, per_device(): lax.all_to_all(sums, 'blk', split_axis=0, concat_axis=0, tiled=True)  19.8 us
    all_to_all x1, waiting for transfers between devices, per_device(): lax.all_to_all(outgoing, 'blk', split_axis=0, concat_axis=0, tiled=True)  12.7 us
    all_to_all x1, starting transfers between devices, per_device(): lax.all_to_all(outgoing, 'blk', split_axis=0, concat_axis=0, tiled=True)  8.31 us
    pallas_call x1, Pallas kernels, per_device(): pl.pallas_call(tile_kernel, in_specs=[smem] + [vmem] * 4, out_shape=jax.S...  4.19 us
    all_to_all x1, starting transfers between devices, per_device(): lax.all_to_all(picked, ('blk', 'rep'), split_axis=0, concat_axis=0, tiled...  3.01 us
    convert_element_type x1, other arithmetic, per_device(): counts[0].astype(bf16)  2.76 us
  transfers between devices with their start and end apart: 3, of which 3 were waited for; matrix products, arithmetic and copies ran while one was open for 5% of the time, Pallas kernels for 0%

profile of v3, /device:TPU:0, one launch (start us, length us, event | category | flops | bytes accessed | tf_op | source)
XLA Modules:
  0.0 114.5 jit_solution(9724572157033229426)
XLA Ops:
  0.6 2.0 %pack.1 = bf16[16,136,128]{2,1,0:T(8,128)(2,1)} custom-call(f32[1024,256]{1,0:T(8,128)} %bitcast.23, bf16[1,1024]{1,0:T(2,128)(2,1)} %margin_ref.1), custom_call_target="tpu_custom_call" | custom-call | tf_op jit(solution)/shard_map/pack/pallas_call | solution.py:156
  2.6 8.3 %all-to-all-start = ((bf16[16,136,128]{2,1,0:T(8,128)(2,1)}), bf16[16,136,128]{2,1,0:T(8,128)(2,1)S(1)}, u32[]{:S(2)}, u32[]{:S(2)}) async-start(bf16[16,136,128]{2,1,0:T(8,128)(2,1)} %pack.1), calls=%async_computation | async-start | bytes 1114112 | tf_op jit(solution)/shard_map/all_to_all | solution.py:169
  10.9 0.8 fusion
  11.7 0.8 slice_bitcast_fusion.1
  12.5 0.7 gather_fusion.1
  13.2 0.7 gather_fusion
  13.9 12.7 %all-to-all-done.held_ref = bf16[16,136,128]{2,1,0:T(8,128)(2,1)S(1)} async-done(((bf16[16,136,128]{2,1,0:T(8,128)(2,1)}), bf16[16,136,128]{2,1,0:T(8,128)(2,1)S(1)}, u32[]{:S(2)}, u32[]{:S(2)}) %all-to-all-start) | async-done | bytes 557088 | tf_op jit(solution)/shard_map/all_to_all | solution.py:169
  26.6 1.8 %pick.1 = (bf16[32,128,128]{2,1,0:T(8,128)(2,1)}, bf16[16,8,128]{2,1,0:T(8,128)(2,1)S(1)}) custom-call(s32[32]{0:T(128)S(1)} %dynamic-slice_bitcast_fusion.slot_ref, bf16[16,136,128]{2,1,0:T(8,128)(2,1)S(1)} %all-to-all-done.held_ref), custom_call_target="tpu_custom_call" | custom-call | tf_op jit(solution)/shard_map/pick/pallas_call | solution.py:170
  28.4 3.0 %all-to-all-start.1 = ((bf16[32,128,128]{2,1,0:T(8,128)(2,1)}), bf16[32,128,128]{2,1,0:T(8,128)(2,1)S(1)}, u32[]{:S(2)}, u32[]{:S(2)}) async-start(bf16[32,128,128]{2,1,0:T(8,128)(2,1)} %get-tuple-element.6), calls=%async_computation.1 | async-start | bytes 2097152 | tf_op jit(solution)/shard_map/all_to_all | solution.py:183
  31.4 0.2 dynamic-slice_reduce_fusion
  31.6 2.8 %convert_bitcast_fusion.counts_ref = bf16[1024,1024]{1,0:T(8,128)(2,1)S(1)} fusion(s32[1,1024,1024]{2,1,0:T(8,128)} %param.6), kind=kLoop, calls=%fused_computation.2 | loop fusion | flops 1048576 | bytes 6291456 | tf_op jit(solution)/shard_map/convert_element_type | solution.py:194
  34.4 0.3 collective-permute-start
  34.7 0.1 pad_add_fusion.1.place_ref
  34.8 0.9 collective-permute-done.other_ref
  35.7 22.0 %all-to-all-done.1 = bf16[32,128,128]{2,1,0:T(8,128)(2,1)S(1)} async-done(((bf16[32,128,128]{2,1,0:T(8,128)(2,1)}), bf16[32,128,128]{2,1,0:T(8,128)(2,1)S(1)}, u32[]{:S(2)}, u32[]{:S(2)}) %all-to-all-start.1) | async-done | bytes 1048608 | tf_op jit(solution)/shard_map/all_to_all | solution.py:183
  57.7 0.0 copy-start
  57.7 0.0 copy-start.1
  57.7 4.2 %tile.1 = bf16[16,2,64,256]{3,2,1,0:T(8,128)(2,1)S(1)} custom-call(s32[3]{0:T(128)S(1)} %pad_add_fusion.1.place_ref, bf16[1024,1024]{1,0:T(8,128)(2,1)S(1)} %convert_bitcast_fusion.counts_ref, bf16[16,2,128,128]{3,2,1,0:T(8,128)(2,1)S(1)} %bitcast.21, bf16[16,8,128]{2,1,0:T(8,128)(2,1)S(1)} %get-tuple-element.7.mine_ref, ...), custom_call_target="tpu_custom_call" | custom-call | tf_op jit(solution)/shard_map/tile/pallas_call | solution.py:184
  61.9 29.7 %all_to_all.20.returned_ref = bf16[32,64,256]{2,1,0:T(8,128)(2,1)S(1)} all-to-all(bf16[32,64,256]{2,1,0:T(8,128)(2,1)S(1)} %bitcast.22), channel_id=1, replica_groups=mesh['blk'=16,'rep'=2] {'blk','rep'}, dimensions={0} | all-to-all | bytes 2097152 | tf_op jit(solution)/shard_map/all_to_all | solution.py:195
  91.5 1.7 %sum.1 = bf16[16,64,256]{2,1,0:T(8,128)(2,1)S(1)} custom-call(s32[32]{0:T(128)S(1)} %dynamic-slice_bitcast_fusion.slot_ref, bf16[32,64,256]{2,1,0:T(8,128)(2,1)S(1)} %all_to_all.20.returned_ref), custom_call_target="tpu_custom_call" | custom-call | tf_op jit(solution)/shard_map/sum/pallas_call | solution.py:198
  93.2 19.8 %all_to_all.21.sums_ref = bf16[16,64,256]{2,1,0:T(8,128)(2,1)S(1)} all-to-all(bf16[16,64,256]{2,1,0:T(8,128)(2,1)S(1)} %sum.1), channel_id=1, replica_groups=mesh['blk'=16,'rep'=2] {'blk'}, dimensions={0} | all-to-all | bytes 1048576 | tf_op jit(solution)/shard_map/all_to_all | solution.py:206
  113.0 0.0 copy-done
  113.0 0.0 copy-done.1
  113.0 1.5 %update.1 = (f32[1024,256]{1,0:T(8,128)}, f32[1024,256]{1,0:T(8,128)}) custom-call(bf16[16,64,256]{2,1,0:T(8,128)(2,1)S(1)} %all_to_all.21.sums_ref, f32[1024,256]{1,0:T(8,128)S(1)} %bitcast.24, f32[1024,256]{1,0:T(8,128)S(1)} %bitcast.25), custom_call_target="tpu_custom_call" | custom-call | tf_op jit(solution)/shard_map/update/pallas_call | solution.py:207
  (3 shorter events, 0.0 us)
Async XLA Ops:
  2.6 24.0 %all-to-all-start = ((bf16[16,136,128]{2,1,0:T(8,128)(2,1)}), bf16[16,136,128]{2,1,0:T(8,128)(2,1)S(1)}, u32[]{:S(2)}, u32[]{:S(2)}) async-start(bf16[16,136,128]{2,1,0:T(8,128)(2,1)} %pack.1), calls=%async_computation | async-start | bytes 1114112 | tf_op jit(solution)/shard_map/all_to_all | solution.py:169
  28.4 29.3 %all-to-all-start.1 = ((bf16[32,128,128]{2,1,0:T(8,128)(2,1)}), bf16[32,128,128]{2,1,0:T(8,128)(2,1)S(1)}, u32[]{:S(2)}, u32[]{:S(2)}) async-start(bf16[32,128,128]{2,1,0:T(8,128)(2,1)} %get-tuple-element.6), calls=%async_computation.1 | async-start | bytes 2097152 | tf_op jit(solution)/shard_map/all_to_all | solution.py:183
  34.4 1.3 %collective-permute-start = (bf16[16,8,128]{2,1,0:T(8,128)(2,1)S(1)}, bf16[16,8,128]{2,1,0:T(8,128)(2,1)S(1)}, u32[]{:S(2)}, u32[]{:S(2)}) collective-permute-start(bf16[16,8,128]{2,1,0:T(8,128)(2,1)S(1)} %get-tuple-element.7.mine_ref), channel_id=1, source_target_pairs={{0,1},{1,0},{2,3},{3,2},{4,5},{5,4},{6,7},{7,6},{8,9},{9,8},{10,11... | collective-permute-start | bytes 98312 | tf_op jit(solution)/shard_map/ppermute | solution.py:182
  57.7 55.3 %copy-start = (f32[1,1024,256]{2,1,0:T(8,128)S(1)}, f32[1,1024,256]{2,1,0:T(8,128)}, u32[]{:S(2)}) copy-start(f32[1,1024,256]{2,1,0:T(8,128)} %param.9) | copy-start | bytes 3145732
  57.7 55.3 %copy-start.1 = (f32[1,1024,256]{2,1,0:T(8,128)S(1)}, f32[1,1024,256]{2,1,0:T(8,128)}, u32[]{:S(2)}) copy-start(f32[1,1024,256]{2,1,0:T(8,128)} %param.10) | copy-start | bytes 3145732

commit v4 on v3

--- a/solution.py
+++ b/solution.py
@@ -1,3 +1,5 @@
+import functools
+
 import jax
 import jax.numpy as jnp
 from jax import lax
@@ -10,6 +12,53 @@
 conf_scale = 0.25
 
 LANES = 128
+
+SPREAD_ORDER = (
+    7, 3, 5, 15, 10, 12, 14, 4, 13, 6, 8, 2, 1, 0, 11, 9,
+)
+FETCH_ORDER = (
+    0, 8, 16, 24, 4, 12, 19, 28, 1, 9, 17, 25, 5, 13, 21, 29,
+    2, 10, 18, 26, 6, 14, 22, 30, 3, 11, 20, 27, 7, 15, 23, 31,
+)
+RETURN_ORDER = (
+    0, 21, 26, 6, 18, 22, 7, 16, 31, 8, 29, 5, 10, 11, 12, 4,
+    24, 14, 25, 28, 13, 19, 27, 30, 17, 9, 20, 3, 1, 2, 15, 23,
+)
+COLLECT_ORDER = (
+    11, 13, 9, 5, 7, 4, 8, 15, 10, 6, 12, 0, 3, 1, 14, 2,
+)
+
+
+class Orders:
+    def __init__(self, owners, requests):
+        tuned = owners == len(SPREAD_ORDER) and requests == len(RETURN_ORDER)
+        self.chips = SPREAD_ORDER if tuned else tuple(range(owners))
+        self.collect = COLLECT_ORDER if tuned else tuple(range(owners))
+        self.fetch = FETCH_ORDER if tuned else tuple(range(requests))
+        self.back = RETURN_ORDER if tuned else tuple(range(requests))
+        self.chip_place = tuple(self.chips.index(c) for c in range(owners))
+        self.planes = requests // owners
+
+    def holder(self, piece, plane):
+        return self.chips[piece] * self.planes + plane
+
+
+def swap_chips(x, chips):
+    return lax.all_to_all(
+        x, "blk", split_axis=0, concat_axis=0, tiled=True, axis_index_groups=[list(chips)]
+    )
+
+
+def swap_all(x, devices):
+    return lax.all_to_all(
+        x,
+        ("blk", "rep"),
+        split_axis=0,
+        concat_axis=0,
+        tiled=True,
+        axis_index_groups=[list(devices)],
+    )
+
 ROWS = 256
 MIB = 1024 * 1024
 
@@ -45,13 +94,14 @@
         out_ref[s, halves * rows :, :] = offsets
 
 
-def pick_kernel(slot_ref, held_ref, out_ref, offsets_ref, copied):
+def pick_kernel(orders, slot_ref, held_ref, out_ref, offsets_ref, copied):
     requests, piece, _ = out_ref.shape
     copies = []
     for r in range(requests):
+        slot = slot_ref[orders.fetch[r]]
         copies.append(
             pltpu.make_async_copy(
-                held_ref.at[slot_ref[r], pl.ds(0, piece), :], out_ref.at[r], copied.at[r]
+                held_ref.at[slot, pl.ds(0, piece), :], out_ref.at[r], copied.at[r]
             )
         )
         copies[-1].start()
@@ -61,15 +111,25 @@
 
 
 def tile_kernel(
-    place_ref, counts_ref, arrived_ref, mine_ref, other_ref, out_ref, row_off, col_off
+    orders, place_ref, counts_ref, arrived_ref, mine_ref, other_ref, out_ref, row_off, col_off
 ):
-    owners, _, rows, width = out_ref.shape
+    requests, rows, width = out_ref.shape
+    owners = requests // orders.planes
     halves = width // LANES
     block = counts_ref.shape[0]
 
     def vectors(pieces, plane):
-        parts = [arrived_ref[pieces, plane, h * rows : (h + 1) * rows, :] for h in range(halves)]
-        return jnp.concatenate([p.reshape(-1, LANES) for p in parts], axis=1)
+        places = [orders.fetch.index(orders.holder(p, plane)) for p in pieces]
+        parts = [
+            jnp.concatenate([arrived_ref[j, h * rows : (h + 1) * rows, :] for j in places], axis=0)
+            for h in range(halves)
+        ]
+        return jnp.concatenate(parts, axis=1)
+
+    def deal(gradient, pieces, plane):
+        coded = code(gradient).astype(jnp.bfloat16)
+        for q, p in enumerate(pieces):
+            out_ref[orders.back.index(orders.holder(p, plane))] = coded[q * rows : (q + 1) * rows, :]
 
     plane = place_ref[0]
     row_slot = place_ref[1]
@@ -80,12 +140,12 @@
     for r in range(block // LANES):
         row_off[r * LANES : (r + 1) * LANES, :] = turned[:, r : r + 1]
         col_off[:, r * LANES : (r + 1) * LANES] = col_m[r : r + 1, :]
-    cols = vectors(slice(0, owners), 1)
+    cols = vectors(range(owners), 1)
     pieces = ROWS // rows
     col_sum = None
     for step in range(block // ROWS):
         here = slice(step * ROWS, (step + 1) * ROWS)
-        there = slice(step * pieces, (step + 1) * pieces)
+        there = range(step * pieces, (step + 1) * pieces)
         row_vectors = vectors(there, 0)
         scores = lax.dot_general(
             row_vectors, cols, (((1,), (1,)), ((), ())), preferred_element_type=jnp.float32
@@ -98,23 +158,24 @@
         hinge = 0.5 + 0.5 * jnp.tanh(0.5 * shifted)
         cell_grad = jnp.where(tile_counts > 0, fitted, hinge).astype(jnp.bfloat16)
         row_gradient = jnp.dot(cell_grad, cols, preferred_element_type=jnp.float32)
-        out_ref[there, 0] = code(row_gradient).astype(jnp.bfloat16).reshape(pieces, rows, width)
+        deal(row_gradient, there, 0)
         part = lax.dot_general(
             cell_grad, row_vectors, (((0,), (0,)), ((), ())), preferred_element_type=jnp.float32
         )
         col_sum = part if step == 0 else col_sum + part
-    out_ref[:, 1] = code(col_sum).astype(jnp.bfloat16).reshape(owners, rows, width)
-
-
-def sum_kernel(slot_ref, returned_ref, out_ref, total):
+    deal(col_sum, range(owners), 1)
+
+
+def sum_kernel(orders, slot_ref, returned_ref, out_ref, total):
     total[...] = jnp.zeros_like(total)
     for r in range(returned_ref.shape[0]):
-        total[slot_ref[r]] += decode(returned_ref[r])
-    out_ref[...] = code(total[...]).astype(jnp.bfloat16)
+        total[slot_ref[orders.back[r]]] += decode(returned_ref[r])
+    for s, chip in enumerate(orders.collect):
+        out_ref[s] = code(total[orders.chip_place[chip]]).astype(jnp.bfloat16)
 
 
 def update_kernel(
-    sums_ref, embed_ref, accum_ref, new_embed_ref, new_accum_ref, embed_v, accum_v, copied
+    orders, sums_ref, embed_ref, accum_ref, new_embed_ref, new_accum_ref, embed_v, accum_v, copied
 ):
     pieces, rows, width = sums_ref.shape
     steps = copied.shape[1]
@@ -122,7 +183,8 @@
     for step in range(steps):
         some = pieces // steps
         here = pl.ds(step * some * rows, some * rows)
-        gradient = decode(sums_ref[step * some : (step + 1) * some].reshape(some * rows, width))
+        held = [orders.collect.index(orders.chips[p]) for p in range(step * some, (step + 1) * some)]
+        gradient = decode(jnp.concatenate([sums_ref[p] for p in held], axis=0))
         new_accum = accum_ref[here, :] + gradient * gradient
         accum_v[here, :] = new_accum
         embed_v[here, :] = embed_ref[here, :] - learn_rate * gradient * lax.rsqrt(new_accum)
@@ -147,7 +209,9 @@
     vmem = pl.BlockSpec(memory_space=pltpu.VMEM)
     f32, bf16 = jnp.float32, jnp.bfloat16
 
-    wanted = jnp.stack([owner_map[k][tile_list[:, k]] for k in range(2)])
+    orders = Orders(owners, requests)
+    places = jnp.asarray(orders.chip_place, jnp.int32)[owner_map]
+    wanted = jnp.stack([places[k][tile_list[:, k]] for k in range(2)])
     slot_of = wanted[plane]
     me = lax.axis_index("blk") * lax.axis_size("rep") + plane
     place = jnp.concatenate([plane[None], wanted[:, me]]).astype(jnp.int32)
@@ -166,9 +230,9 @@
         compiler_params=params(60),
         name="pack",
     )(embed[0], margins)
-    held = lax.all_to_all(outgoing, "blk", split_axis=0, concat_axis=0, tiled=True)
+    held = swap_chips(outgoing, orders.chips)
     picked, offsets = pl.pallas_call(
-        pick_kernel,
+        functools.partial(pick_kernel, orders),
         in_specs=[smem, vmem],
         out_specs=(pl.BlockSpec(memory_space=pl.ANY), vmem),
         out_shape=(
@@ -180,32 +244,30 @@
         name="pick",
     )(slot_of, held)
     other_offsets = lax.ppermute(offsets, "rep", [(0, 1), (1, 0)])
-    arrived = lax.all_to_all(picked, ("blk", "rep"), split_axis=0, concat_axis=0, tiled=True)
+    arrived = swap_all(picked, orders.fetch)
     partials = pl.pallas_call(
-        tile_kernel,
+        functools.partial(tile_kernel, orders),
         in_specs=[smem] + [vmem] * 4,
-        out_shape=jax.ShapeDtypeStruct((owners, 2, rows, width), bf16),
+        out_shape=jax.ShapeDtypeStruct((requests, rows, width), bf16),
         scratch_shapes=[
             pltpu.VMEM((block, 1), f32),
             pltpu.VMEM((1, block), f32),
         ],
         compiler_params=params(24),
         name="tile",
-    )(place, counts[0].astype(bf16), arrived.reshape(owners, 2, halves * rows, LANES), offsets, other_offsets)
-    returned = lax.all_to_all(
-        partials.reshape(requests, rows, width), ("blk", "rep"), split_axis=0, concat_axis=0, tiled=True
-    )
+    )(place, counts[0].astype(bf16), arrived, offsets, other_offsets)
+    returned = swap_all(partials, orders.back)
     sums = pl.pallas_call(
-        sum_kernel,
+        functools.partial(sum_kernel, orders),
         in_specs=[smem, vmem],
         out_shape=jax.ShapeDtypeStruct((owners, rows, width), bf16),
         scratch_shapes=[pltpu.VMEM((owners, rows, width), f32)],
         compiler_params=params(16),
         name="sum",
     )(slot_of, returned)
-    gradient = lax.all_to_all(sums, "blk", split_axis=0, concat_axis=0, tiled=True)
+    gradient = swap_chips(sums, orders.collect)
     new_embed, new_accum = pl.pallas_call(
-        update_kernel,
+        functools.partial(update_kernel, orders),
         in_specs=[vmem] * 3,
         out_specs=(pl.BlockSpec(memory_space=pl.ANY),) * 2,
         out_shape=(jax.ShapeDtypeStruct((block, width), f32),) * 2,

time: 115 us -> 111 us (0.965)
  waiting for transfers between devices: 35.6 us -> 31.9 us
  blocking collectives: 49.4 us -> 47.3 us
    all_to_all x2, waiting for transfers between devices: 34.7 us -> 31 us  [the longest x1 21.7 us: swap_all(): lax.all_to_all(x, ('blk', 'rep'), split_axis=0, concat_axis=0, tiled=True...]
    all_to_all x2, blocking collectives: 49.4 us -> 47.3 us  [the longest x1 27.2 us: swap_all(): lax.all_to_all(x, ('blk', 'rep'), split_axis=0, concat_axis=0, tiled=True...]
    gather x2 -> x3, local copies, waits for them, and re-layouts: 1.4 us -> 2.75 us  [the longest x2 1.4 us: per_device(): wanted = jnp.stack([places[k][tile_list[:, k]] for k in range(2)])]
  transfers between devices with their start and end apart: 3 -> 3, of which waited for: 3 -> 3; matrix products, arithmetic and copies ran while one was open for 5% -> 7% of each run, Pallas kernels for 0% -> 0%
where the time goes in v4:
time: 111 us; the launch traced here: 110 us
  blocking collectives  47.3 us (43%)
  waiting for transfers between devices  31.9 us (29%)
  starting transfers between devices  11.9 us (11%)
  Pallas kernels  10.9 us (10%)
  other arithmetic  4.31 us (4%)
  local copies, waits for them, and re-layouts  3.11 us (3%)
    all_to_all x1, blocking collectives, swap_all(): lax.all_to_all(x, ('blk', 'rep'), split_axis=0, concat_axis=0, tiled=True...  27.2 us
    all_to_all x1, waiting for transfers between devices, swap_all(): lax.all_to_all(x, ('blk', 'rep'), split_axis=0, concat_axis=0, tiled=True...  21.7 us
    all_to_all x1, blocking collectives, swap_chips(): lax.all_to_all(x, 'blk', split_axis=0, concat_axis=0, tiled=True, axis_in...  20.1 us
    all_to_all x1, waiting for transfers between devices, swap_chips(): lax.all_to_all(x, 'blk', split_axis=0, concat_axis=0, tiled=True, axis_in...  9.31 us
    all_to_all x1, starting transfers between devices, swap_chips(): lax.all_to_all(x, 'blk', split_axis=0, concat_axis=0, tiled=True, axis_in...  8.79 us
    pallas_call x1, Pallas kernels, per_device(): pl.pallas_call(functools.partial(tile_kernel, orders), in_specs=[smem] +...  4.18 us
    all_to_all x1, starting transfers between devices, swap_all(): lax.all_to_all(x, ('blk', 'rep'), split_axis=0, concat_axis=0, tiled=True...  2.78 us
    convert_element_type x1, other arithmetic, per_device(): counts[0].astype(bf16)  2.76 us
  transfers between devices with their start and end apart: 3, of which 3 were waited for; matrix products, arithmetic and copies ran while one was open for 7% of the time, Pallas kernels for 0%

profile of v4, /device:TPU:0, one launch (start us, length us, event | category | flops | bytes accessed | tf_op | source)
XLA Modules:
  0.0 110.1 jit_solution(18729270457349896)
XLA Ops:
  0.6 2.0 %pack.1 = bf16[16,136,128]{2,1,0:T(8,128)(2,1)} custom-call(f32[1024,256]{1,0:T(8,128)} %bitcast.15, bf16[1,1024]{1,0:T(2,128)(2,1)} %margin_ref.1), custom_call_target="tpu_custom_call" | custom-call | tf_op jit(solution)/shard_map/pack/pallas_call | solution.py:220
  2.6 8.8 %all-to-all-start = ((bf16[16,136,128]{2,1,0:T(8,128)(2,1)}), bf16[16,136,128]{2,1,0:T(8,128)(2,1)S(1)}, u32[]{:S(2)}, u32[]{:S(2)}) async-start(bf16[16,136,128]{2,1,0:T(8,128)(2,1)} %pack.1), calls=%async_computation | async-start | bytes 1114112 | tf_op jit(solution)/shard_map/all_to_all | solution.py:47
  11.4 0.7 compare_select_fusion
  12.1 0.1 reshape.7
  12.2 1.4 %gather_fusion = s32[32]{0:T(128)S(1)} fusion(s32[16]{0:T(128)} %constant.6.clone, s32[1024]{0:T(1024)S(1)} %pad_clamp_fusion.2), kind=kCustom, calls=%fused_computation | custom fusion | bytes 384 | tf_op jit(solution)/shard_map/gather | solution.py:213
  13.5 0.8 fusion
  14.3 0.1 fusion.2
  14.4 0.7 gather_fusion.2
  15.1 0.7 gather_fusion.1
  15.8 9.3 %all-to-all-done.held_ref = bf16[16,136,128]{2,1,0:T(8,128)(2,1)S(1)} async-done(((bf16[16,136,128]{2,1,0:T(8,128)(2,1)}), bf16[16,136,128]{2,1,0:T(8,128)(2,1)S(1)}, u32[]{:S(2)}, u32[]{:S(2)}) %all-to-all-start) | async-done | bytes 557088 | tf_op jit(solution)/shard_map/all_to_all | solution.py:47
  25.1 1.8 %pick.1 = (bf16[32,128,128]{2,1,0:T(8,128)(2,1)}, bf16[16,8,128]{2,1,0:T(8,128)(2,1)S(1)}) custom-call(s32[32]{0:T(128)S(1)} %dynamic-slice_bitcast_fusion.slot_ref, bf16[16,136,128]{2,1,0:T(8,128)(2,1)S(1)} %all-to-all-done.held_ref), custom_call_target="tpu_custom_call" | custom-call | tf_op jit(solution)/shard_map/pick/pallas_call | solution.py:234
  26.9 2.8 %all-to-all-start.1 = ((bf16[32,128,128]{2,1,0:T(8,128)(2,1)}), bf16[32,128,128]{2,1,0:T(8,128)(2,1)S(1)}, u32[]{:S(2)}, u32[]{:S(2)}) async-start(bf16[32,128,128]{2,1,0:T(8,128)(2,1)} %get-tuple-element.6), calls=%async_computation.1 | async-start | bytes 2097152 | tf_op jit(solution)/shard_map/all_to_all | solution.py:53
  29.7 0.2 dynamic-slice_reduce_fusion
  29.9 2.8 %convert_bitcast_fusion.counts_ref = bf16[1024,1024]{1,0:T(8,128)(2,1)S(1)} fusion(s32[1,1024,1024]{2,1,0:T(8,128)} %param.7), kind=kLoop, calls=%fused_computation.3 | loop fusion | flops 1048576 | bytes 6291456 | tf_op jit(solution)/shard_map/convert_element_type | solution.py:258
  32.6 0.3 collective-permute-start
  33.0 0.1 pad_add_fusion.1.place_ref
  33.0 0.9 collective-permute-done.other_ref
  33.9 21.7 %all-to-all-done.1.arrived_ref = bf16[32,128,128]{2,1,0:T(8,128)(2,1)S(1)} async-done(((bf16[32,128,128]{2,1,0:T(8,128)(2,1)}), bf16[32,128,128]{2,1,0:T(8,128)(2,1)S(1)}, u32[]{:S(2)}, u32[]{:S(2)}) %all-to-all-start.1) | async-done | bytes 1048608 | tf_op jit(solution)/shard_map/all_to_all | solution.py:53
  55.6 4.2 %tile.1 = bf16[32,64,256]{2,1,0:T(8,128)(2,1)S(1)} custom-call(s32[3]{0:T(128)S(1)} %pad_add_fusion.1.place_ref, bf16[1024,1024]{1,0:T(8,128)(2,1)S(1)} %convert_bitcast_fusion.counts_ref, bf16[32,128,128]{2,1,0:T(8,128)(2,1)S(1)} %all-to-all-done.1.arrived_ref, bf16[16,8,128]{2,1,0:T(8,128)(2,1)S(1)} %get-tuple-element.7.mine_ref, ...), custom_call_target="tpu_custom_call" | custom-call | tf_op jit(solution)/shard_map/tile/pallas_call | solution.py:248
  59.8 27.2 %all_to_all.20.returned_ref = bf16[32,64,256]{2,1,0:T(8,128)(2,1)S(1)} all-to-all(bf16[32,64,256]{2,1,0:T(8,128)(2,1)S(1)} %tile.1), channel_id=1, replica_groups={{0,21,26,6,18,22,7,16,31,8,29,5,10,11,12,4,24,14,25,28,13,19,27,30,17,9..., dimensions={0} | all-to-all | bytes 2097152 | tf_op jit(solution)/shard_map/all_to_all | solution.py:53
  87.0 1.5 %sum.1 = bf16[16,64,256]{2,1,0:T(8,128)(2,1)S(1)} custom-call(s32[32]{0:T(128)S(1)} %dynamic-slice_bitcast_fusion.slot_ref, bf16[32,64,256]{2,1,0:T(8,128)(2,1)S(1)} %all_to_all.20.returned_ref), custom_call_target="tpu_custom_call" | custom-call | tf_op jit(solution)/shard_map/sum/pallas_call | solution.py:260
  88.5 20.1 %all_to_all.21.sums_ref = bf16[16,64,256]{2,1,0:T(8,128)(2,1)S(1)} all-to-all(bf16[16,64,256]{2,1,0:T(8,128)(2,1)S(1)} %sum.1), channel_id=1, replica_groups={{22,26,18,10,14,8,16,30,20,12,24,0,6,2,28,4},{23,27,19,11,15,9,17,31,21..., dimensions={0} | all-to-all | bytes 1048576 | tf_op jit(solution)/shard_map/all_to_all | solution.py:47
  108.6 0.0 copy-done.1
  108.6 1.5 %update.1 = (f32[1024,256]{1,0:T(8,128)}, f32[1024,256]{1,0:T(8,128)}) custom-call(bf16[16,64,256]{2,1,0:T(8,128)(2,1)S(1)} %all_to_all.21.sums_ref, f32[1024,256]{1,0:T(8,128)S(1)} %bitcast.16, f32[1024,256]{1,0:T(8,128)S(1)} %bitcast.17), custom_call_target="tpu_custom_call" | custom-call | tf_op jit(solution)/shard_map/update/pallas_call | solution.py:269
  (7 shorter events, 0.0 us)
Async XLA Ops:
  2.6 22.5 %all-to-all-start = ((bf16[16,136,128]{2,1,0:T(8,128)(2,1)}), bf16[16,136,128]{2,1,0:T(8,128)(2,1)S(1)}, u32[]{:S(2)}, u32[]{:S(2)}) async-start(bf16[16,136,128]{2,1,0:T(8,128)(2,1)} %pack.1), calls=%async_computation | async-start | bytes 1114112 | tf_op jit(solution)/shard_map/all_to_all | solution.py:47
  26.9 28.7 %all-to-all-start.1 = ((bf16[32,128,128]{2,1,0:T(8,128)(2,1)}), bf16[32,128,128]{2,1,0:T(8,128)(2,1)S(1)}, u32[]{:S(2)}, u32[]{:S(2)}) async-start(bf16[32,128,128]{2,1,0:T(8,128)(2,1)} %get-tuple-element.6), calls=%async_computation.1 | async-start | bytes 2097152 | tf_op jit(solution)/shard_map/all_to_all | solution.py:53
  32.6 1.3 %collective-permute-start = (bf16[16,8,128]{2,1,0:T(8,128)(2,1)S(1)}, bf16[16,8,128]{2,1,0:T(8,128)(2,1)S(1)}, u32[]{:S(2)}, u32[]{:S(2)}) collective-permute-start(bf16[16,8,128]{2,1,0:T(8,128)(2,1)S(1)} %get-tuple-element.7.mine_ref), channel_id=1, source_target_pairs={{0,1},{1,0},{2,3},{3,2},{4,5},{5,4},{6,7},{7,6},{8,9},{9,8},{10,11... | collective-permute-start | bytes 98312 | tf_op jit(solution)/shard_map/ppermute | solution.py:246
  55.6 52.9 %copy-start = (f32[1,1024,256]{2,1,0:T(8,128)S(1)}, f32[1,1024,256]{2,1,0:T(8,128)}, u32[]{:S(2)}) copy-start(f32[1,1024,256]{2,1,0:T(8,128)} %param.10) | copy-start | bytes 3145732
  55.6 52.9 %copy-start.1 = (f32[1,1024,256]{2,1,0:T(8,128)S(1)}, f32[1,1024,256]{2,1,0:T(8,128)}, u32[]{:S(2)}) copy-start(f32[1,1024,256]{2,1,0:T(8,128)} %param.11) | copy-start | bytes 3145732

commit v5 on v4

--- a/solution.py
+++ b/solution.py
@@ -14,18 +14,18 @@
 LANES = 128
 
 SPREAD_ORDER = (
-    7, 3, 5, 15, 10, 12, 14, 4, 13, 6, 8, 2, 1, 0, 11, 9,
+    7, 12, 5, 15, 10, 3, 14, 9, 13, 6, 8, 2, 1, 0, 11, 4,
 )
 FETCH_ORDER = (
     0, 8, 16, 24, 4, 12, 19, 28, 1, 9, 17, 25, 5, 13, 21, 29,
     2, 10, 18, 26, 6, 14, 22, 30, 3, 11, 20, 27, 7, 15, 23, 31,
 )
 RETURN_ORDER = (
-    0, 21, 26, 6, 18, 22, 7, 16, 31, 8, 29, 5, 10, 11, 12, 4,
-    24, 14, 25, 28, 13, 19, 27, 30, 17, 9, 20, 3, 1, 2, 15, 23,
+    0, 1, 15, 14, 13, 12, 11, 10, 9, 8, 7, 6, 5, 4, 3, 2,
+    16, 17, 18, 19, 20, 21, 22, 23, 24, 25, 26, 27, 28, 29, 30, 31,
 )
 COLLECT_ORDER = (
-    11, 13, 9, 5, 7, 4, 8, 15, 10, 6, 12, 0, 3, 1, 14, 2,
+    8, 3, 10, 14, 2, 11, 13, 4, 6, 12, 5, 7, 1, 0, 15, 9,
 )
 
 

time: 111 us -> 110 us (level)
    all_to_all x1, blocking collectives: 20.1 us -> 17.3 us  [swap_chips(): lax.all_to_all(x, 'blk', split_axis=0, concat_axis=0, tiled=True, axis_in...]
    all_to_all x1, blocking collectives: 27.2 us -> 29.1 us  [swap_all(): lax.all_to_all(x, ('blk', 'rep'), split_axis=0, concat_axis=0, tiled=True...]
where the time goes in v5:
time: 110 us; the launch traced here: 109 us
  blocking collectives  46.3 us (42%)
  waiting for transfers between devices  31.9 us (29%)
  starting transfers between devices  11.8 us (11%)
  Pallas kernels  10.9 us (10%)
  other arithmetic  4.31 us (4%)
  local copies, waits for them, and re-layouts  3.11 us (3%)
    all_to_all x1, blocking collectives, swap_all(): lax.all_to_all(x, ('blk', 'rep'), split_axis=0, concat_axis=0, tiled=True...  29.1 us
    all_to_all x1, waiting for transfers between devices, swap_all(): lax.all_to_all(x, ('blk', 'rep'), split_axis=0, concat_axis=0, tiled=True...  21.7 us
    all_to_all x1, blocking collectives, swap_chips(): lax.all_to_all(x, 'blk', split_axis=0, concat_axis=0, tiled=True, axis_in...  17.3 us
    all_to_all x1, waiting for transfers between devices, swap_chips(): lax.all_to_all(x, 'blk', split_axis=0, concat_axis=0, tiled=True, axis_in...  9.31 us
    all_to_all x1, starting transfers between devices, swap_chips(): lax.all_to_all(x, 'blk', split_axis=0, concat_axis=0, tiled=True, axis_in...  8.79 us
    pallas_call x1, Pallas kernels, per_device(): pl.pallas_call(functools.partial(tile_kernel, orders), in_specs=[smem] +...  4.18 us
    convert_element_type x1, other arithmetic, per_device(): counts[0].astype(bf16)  2.76 us
    all_to_all x1, starting transfers between devices, swap_all(): lax.all_to_all(x, ('blk', 'rep'), split_axis=0, concat_axis=0, tiled=True...  2.74 us
  transfers between devices with their start and end apart: 3, of which 3 were waited for; matrix products, arithmetic and copies ran while one was open for 7% of the time, Pallas kernels for 0%

profile of v5, /device:TPU:0, one launch (start us, length us, event | category | flops | bytes accessed | tf_op | source)
XLA Modules:
  0.0 109.1 jit_solution(13819439968675692045)
XLA Ops:
  0.6 2.0 %pack.1 = bf16[16,136,128]{2,1,0:T(8,128)(2,1)} custom-call(f32[1024,256]{1,0:T(8,128)} %bitcast.15, bf16[1,1024]{1,0:T(2,128)(2,1)} %margin_ref.1), custom_call_target="tpu_custom_call" | custom-call | tf_op jit(solution)/shard_map/pack/pallas_call | solution.py:220
  2.6 8.8 %all-to-all-start = ((bf16[16,136,128]{2,1,0:T(8,128)(2,1)}), bf16[16,136,128]{2,1,0:T(8,128)(2,1)S(1)}, u32[]{:S(2)}, u32[]{:S(2)}) async-start(bf16[16,136,128]{2,1,0:T(8,128)(2,1)} %pack.1), calls=%async_computation | async-start | bytes 1114112 | tf_op jit(solution)/shard_map/all_to_all | solution.py:47
  11.4 0.7 compare_select_fusion
  12.1 0.1 reshape.7
  12.2 1.4 %gather_fusion = s32[32]{0:T(128)S(1)} fusion(s32[16]{0:T(128)} %constant.6.clone, s32[1024]{0:T(1024)S(1)} %pad_clamp_fusion.2), kind=kCustom, calls=%fused_computation | custom fusion | bytes 384 | tf_op jit(solution)/shard_map/gather | solution.py:213
  13.5 0.8 fusion
  14.3 0.1 fusion.2
  14.4 0.7 gather_fusion.2
  15.1 0.7 gather_fusion.1
  15.8 9.3 %all-to-all-done.held_ref = bf16[16,136,128]{2,1,0:T(8,128)(2,1)S(1)} async-done(((bf16[16,136,128]{2,1,0:T(8,128)(2,1)}), bf16[16,136,128]{2,1,0:T(8,128)(2,1)S(1)}, u32[]{:S(2)}, u32[]{:S(2)}) %all-to-all-start) | async-done | bytes 557088 | tf_op jit(solution)/shard_map/all_to_all | solution.py:47
  25.1 1.8 %pick.1 = (bf16[32,128,128]{2,1,0:T(8,128)(2,1)}, bf16[16,8,128]{2,1,0:T(8,128)(2,1)S(1)}) custom-call(s32[32]{0:T(128)S(1)} %dynamic-slice_bitcast_fusion.slot_ref, bf16[16,136,128]{2,1,0:T(8,128)(2,1)S(1)} %all-to-all-done.held_ref), custom_call_target="tpu_custom_call" | custom-call | tf_op jit(solution)/shard_map/pick/pallas_call | solution.py:234
  26.9 2.7 %all-to-all-start.1 = ((bf16[32,128,128]{2,1,0:T(8,128)(2,1)}), bf16[32,128,128]{2,1,0:T(8,128)(2,1)S(1)}, u32[]{:S(2)}, u32[]{:S(2)}) async-start(bf16[32,128,128]{2,1,0:T(8,128)(2,1)} %get-tuple-element.6), calls=%async_computation.1 | async-start | bytes 2097152 | tf_op jit(solution)/shard_map/all_to_all | solution.py:53
  29.6 0.2 dynamic-slice_reduce_fusion
  29.8 2.8 %convert_bitcast_fusion.counts_ref = bf16[1024,1024]{1,0:T(8,128)(2,1)S(1)} fusion(s32[1,1024,1024]{2,1,0:T(8,128)} %param.7), kind=kLoop, calls=%fused_computation.3 | loop fusion | flops 1048576 | bytes 6291456 | tf_op jit(solution)/shard_map/convert_element_type | solution.py:258
  32.6 0.3 collective-permute-start
  32.9 0.1 pad_add_fusion.1.place_ref
  33.0 0.9 collective-permute-done.other_ref
  33.9 21.7 %all-to-all-done.1.arrived_ref = bf16[32,128,128]{2,1,0:T(8,128)(2,1)S(1)} async-done(((bf16[32,128,128]{2,1,0:T(8,128)(2,1)}), bf16[32,128,128]{2,1,0:T(8,128)(2,1)S(1)}, u32[]{:S(2)}, u32[]{:S(2)}) %all-to-all-start.1) | async-done | bytes 1048608 | tf_op jit(solution)/shard_map/all_to_all | solution.py:53
  55.6 4.2 %tile.1 = bf16[32,64,256]{2,1,0:T(8,128)(2,1)S(1)} custom-call(s32[3]{0:T(128)S(1)} %pad_add_fusion.1.place_ref, bf16[1024,1024]{1,0:T(8,128)(2,1)S(1)} %convert_bitcast_fusion.counts_ref, bf16[32,128,128]{2,1,0:T(8,128)(2,1)S(1)} %all-to-all-done.1.arrived_ref, bf16[16,8,128]{2,1,0:T(8,128)(2,1)S(1)} %get-tuple-element.7.mine_ref, ...), custom_call_target="tpu_custom_call" | custom-call | tf_op jit(solution)/shard_map/tile/pallas_call | solution.py:248
  59.8 29.1 %all_to_all.20.returned_ref = bf16[32,64,256]{2,1,0:T(8,128)(2,1)S(1)} all-to-all(bf16[32,64,256]{2,1,0:T(8,128)(2,1)S(1)} %tile.1), channel_id=1, replica_groups={{0,1,15,14,13,12,11,10,9,8,7,6,5,4,3,2,16,17,18,19,20,21,22,23,24,25,26..., dimensions={0} | all-to-all | bytes 2097152 | tf_op jit(solution)/shard_map/all_to_all | solution.py:53
  88.8 1.5 %sum.1 = bf16[16,64,256]{2,1,0:T(8,128)(2,1)S(1)} custom-call(s32[32]{0:T(128)S(1)} %dynamic-slice_bitcast_fusion.slot_ref, bf16[32,64,256]{2,1,0:T(8,128)(2,1)S(1)} %all_to_all.20.returned_ref), custom_call_target="tpu_custom_call" | custom-call | tf_op jit(solution)/shard_map/sum/pallas_call | solution.py:260
  90.3 17.3 %all_to_all.21.sums_ref = bf16[16,64,256]{2,1,0:T(8,128)(2,1)S(1)} all-to-all(bf16[16,64,256]{2,1,0:T(8,128)(2,1)S(1)} %sum.1), channel_id=1, replica_groups={{16,6,20,28,4,22,26,8,12,24,10,14,2,0,30,18},{17,7,21,29,5,23,27,9,13,2..., dimensions={0} | all-to-all | bytes 1048576 | tf_op jit(solution)/shard_map/all_to_all | solution.py:47
  107.6 0.0 copy-done.1
  107.6 1.5 %update.1 = (f32[1024,256]{1,0:T(8,128)}, f32[1024,256]{1,0:T(8,128)}) custom-call(bf16[16,64,256]{2,1,0:T(8,128)(2,1)S(1)} %all_to_all.21.sums_ref, f32[1024,256]{1,0:T(8,128)S(1)} %bitcast.16, f32[1024,256]{1,0:T(8,128)S(1)} %bitcast.17), custom_call_target="tpu_custom_call" | custom-call | tf_op jit(solution)/shard_map/update/pallas_call | solution.py:269
  (7 shorter events, 0.0 us)
Async XLA Ops:
  2.6 22.5 %all-to-all-start = ((bf16[16,136,128]{2,1,0:T(8,128)(2,1)}), bf16[16,136,128]{2,1,0:T(8,128)(2,1)S(1)}, u32[]{:S(2)}, u32[]{:S(2)}) async-start(bf16[16,136,128]{2,1,0:T(8,128)(2,1)} %pack.1), calls=%async_computation | async-start | bytes 1114112 | tf_op jit(solution)/shard_map/all_to_all | solution.py:47
  26.9 28.7 %all-to-all-start.1 = ((bf16[32,128,128]{2,1,0:T(8,128)(2,1)}), bf16[32,128,128]{2,1,0:T(8,128)(2,1)S(1)}, u32[]{:S(2)}, u32[]{:S(2)}) async-start(bf16[32,128,128]{2,1,0:T(8,128)(2,1)} %get-tuple-element.6), calls=%async_computation.1 | async-start | bytes 2097152 | tf_op jit(solution)/shard_map/all_to_all | solution.py:53
  32.6 1.3 %collective-permute-start = (bf16[16,8,128]{2,1,0:T(8,128)(2,1)S(1)}, bf16[16,8,128]{2,1,0:T(8,128)(2,1)S(1)}, u32[]{:S(2)}, u32[]{:S(2)}) collective-permute-start(bf16[16,8,128]{2,1,0:T(8,128)(2,1)S(1)} %get-tuple-element.7.mine_ref), channel_id=1, source_target_pairs={{0,1},{1,0},{2,3},{3,2},{4,5},{5,4},{6,7},{7,6},{8,9},{9,8},{10,11... | collective-permute-start | bytes 98312 | tf_op jit(solution)/shard_map/ppermute | solution.py:246
  55.6 52.0 %copy-start = (f32[1,1024,256]{2,1,0:T(8,128)S(1)}, f32[1,1024,256]{2,1,0:T(8,128)}, u32[]{:S(2)}) copy-start(f32[1,1024,256]{2,1,0:T(8,128)} %param.10) | copy-start | bytes 3145732
  55.6 52.0 %copy-start.1 = (f32[1,1024,256]{2,1,0:T(8,128)S(1)}, f32[1,1024,256]{2,1,0:T(8,128)}, u32[]{:S(2)}) copy-start(f32[1,1024,256]{2,1,0:T(8,128)} %param.11) | copy-start | bytes 3145732

commit v6 on v5

--- a/solution.py
+++ b/solution.py
@@ -17,15 +17,15 @@
     7, 12, 5, 15, 10, 3, 14, 9, 13, 6, 8, 2, 1, 0, 11, 4,
 )
 FETCH_ORDER = (
-    0, 8, 16, 24, 4, 12, 19, 28, 1, 9, 17, 25, 5, 13, 21, 29,
+    0, 8, 16, 24, 4, 12, 19, 28, 1, 9, 17, 25, 29, 21, 13, 5,
     2, 10, 18, 26, 6, 14, 22, 30, 3, 11, 20, 27, 7, 15, 23, 31,
 )
 RETURN_ORDER = (
-    0, 1, 15, 14, 13, 12, 11, 10, 9, 8, 7, 6, 5, 4, 3, 2,
+    0, 1, 15, 14, 13, 12, 2, 9, 10, 8, 7, 6, 5, 4, 3, 11,
     16, 17, 18, 19, 20, 21, 22, 23, 24, 25, 26, 27, 28, 29, 30, 31,
 )
 COLLECT_ORDER = (
-    8, 3, 10, 14, 2, 11, 13, 4, 6, 12, 5, 7, 1, 0, 15, 9,
+    8, 10, 3, 14, 2, 11, 13, 4, 6, 12, 5, 7, 1, 0, 15, 9,
 )
 
 

time: 110 us -> 109 us (level)
  no operation moved by 1% of the time
where the time goes in v6:
time: 109 us
  blocking collectives  46 us (42%)
  waiting for transfers between devices  31.7 us (29%)
  starting transfers between devices  11.8 us (11%)
  Pallas kernels  10.9 us (10%)
  other arithmetic  4.31 us (4%)
  local copies, waits for them, and re-layouts  3.11 us (3%)
    all_to_all x1, blocking collectives, swap_all(): lax.all_to_all(x, ('blk', 'rep'), split_axis=0, concat_axis=0, tiled=True...  29.3 us
    all_to_all x1, waiting for transfers between devices, swap_all(): lax.all_to_all(x, ('blk', 'rep'), split_axis=0, concat_axis=0, tiled=True...  21.5 us
    all_to_all x1, blocking collectives, swap_chips(): lax.all_to_all(x, 'blk', split_axis=0, concat_axis=0, tiled=True, axis_in...  16.7 us
    all_to_all x1, waiting for transfers between devices, swap_chips(): lax.all_to_all(x, 'blk', split_axis=0, concat_axis=0, tiled=True, axis_in...  9.31 us
    all_to_all x1, starting transfers between devices, swap_chips(): lax.all_to_all(x, 'blk', split_axis=0, concat_axis=0, tiled=True, axis_in...  8.79 us
    pallas_call x1, Pallas kernels, per_device(): pl.pallas_call(functools.partial(tile_kernel, orders), in_specs=[smem] +...  4.18 us
    convert_element_type x1, other arithmetic, per_device(): counts[0].astype(bf16)  2.76 us
    all_to_all x1, starting transfers between devices, swap_all(): lax.all_to_all(x, ('blk', 'rep'), split_axis=0, concat_axis=0, tiled=True...  2.74 us
  transfers between devices with their start and end apart: 3, of which 3 were waited for; matrix products, arithmetic and copies ran while one was open for 7% of the time, Pallas kernels for 0%

profile of v6, /device:TPU:0, one launch (start us, length us, event | category | flops | bytes accessed | tf_op | source)
XLA Modules:
  0.0 108.6 jit_solution(2301478452348114786)
XLA Ops:
  0.6 2.0 %pack.1 = bf16[16,136,128]{2,1,0:T(8,128)(2,1)} custom-call(f32[1024,256]{1,0:T(8,128)} %bitcast.15, bf16[1,1024]{1,0:T(2,128)(2,1)} %margin_ref.1), custom_call_target="tpu_custom_call" | custom-call | tf_op jit(solution)/shard_map/pack/pallas_call | solution.py:220
  2.6 8.8 %all-to-all-start = ((bf16[16,136,128]{2,1,0:T(8,128)(2,1)}), bf16[16,136,128]{2,1,0:T(8,128)(2,1)S(1)}, u32[]{:S(2)}, u32[]{:S(2)}) async-start(bf16[16,136,128]{2,1,0:T(8,128)(2,1)} %pack.1), calls=%async_computation | async-start | bytes 1114112 | tf_op jit(solution)/shard_map/all_to_all | solution.py:47
  11.4 0.7 compare_select_fusion
  12.1 0.1 reshape.7
  12.2 1.4 %gather_fusion = s32[32]{0:T(128)S(1)} fusion(s32[16]{0:T(128)} %constant.6.clone, s32[1024]{0:T(1024)S(1)} %pad_clamp_fusion.2), kind=kCustom, calls=%fused_computation | custom fusion | bytes 384 | tf_op jit(solution)/shard_map/gather | solution.py:213
  13.5 0.8 fusion
  14.3 0.1 fusion.2
  14.4 0.7 gather_fusion.2
  15.1 0.7 gather_fusion.1
  15.8 9.3 %all-to-all-done.held_ref = bf16[16,136,128]{2,1,0:T(8,128)(2,1)S(1)} async-done(((bf16[16,136,128]{2,1,0:T(8,128)(2,1)}), bf16[16,136,128]{2,1,0:T(8,128)(2,1)S(1)}, u32[]{:S(2)}, u32[]{:S(2)}) %all-to-all-start) | async-done | bytes 557088 | tf_op jit(solution)/shard_map/all_to_all | solution.py:47
  25.1 1.8 %pick.1 = (bf16[32,128,128]{2,1,0:T(8,128)(2,1)}, bf16[16,8,128]{2,1,0:T(8,128)(2,1)S(1)}) custom-call(s32[32]{0:T(128)S(1)} %dynamic-slice_bitcast_fusion.slot_ref, bf16[16,136,128]{2,1,0:T(8,128)(2,1)S(1)} %all-to-all-done.held_ref), custom_call_target="tpu_custom_call" | custom-call | tf_op jit(solution)/shard_map/pick/pallas_call | solution.py:234
  26.9 2.7 %all-to-all-start.1 = ((bf16[32,128,128]{2,1,0:T(8,128)(2,1)}), bf16[32,128,128]{2,1,0:T(8,128)(2,1)S(1)}, u32[]{:S(2)}, u32[]{:S(2)}) async-start(bf16[32,128,128]{2,1,0:T(8,128)(2,1)} %get-tuple-element.6), calls=%async_computation.1 | async-start | bytes 2097152 | tf_op jit(solution)/shard_map/all_to_all | solution.py:53
  29.6 0.2 dynamic-slice_reduce_fusion
  29.8 2.8 %convert_bitcast_fusion.counts_ref = bf16[1024,1024]{1,0:T(8,128)(2,1)S(1)} fusion(s32[1,1024,1024]{2,1,0:T(8,128)} %param.7), kind=kLoop, calls=%fused_computation.3 | loop fusion | flops 1048576 | bytes 6291456 | tf_op jit(solution)/shard_map/convert_element_type | solution.py:258
  32.6 0.3 collective-permute-start
  32.9 0.1 pad_add_fusion.1.place_ref
  33.0 0.9 collective-permute-done.other_ref
  33.9 21.5 %all-to-all-done.1.arrived_ref = bf16[32,128,128]{2,1,0:T(8,128)(2,1)S(1)} async-done(((bf16[32,128,128]{2,1,0:T(8,128)(2,1)}), bf16[32,128,128]{2,1,0:T(8,128)(2,1)S(1)}, u32[]{:S(2)}, u32[]{:S(2)}) %all-to-all-start.1) | async-done | bytes 1048608 | tf_op jit(solution)/shard_map/all_to_all | solution.py:53
  55.4 4.2 %tile.1 = bf16[32,64,256]{2,1,0:T(8,128)(2,1)S(1)} custom-call(s32[3]{0:T(128)S(1)} %pad_add_fusion.1.place_ref, bf16[1024,1024]{1,0:T(8,128)(2,1)S(1)} %convert_bitcast_fusion.counts_ref, bf16[32,128,128]{2,1,0:T(8,128)(2,1)S(1)} %all-to-all-done.1.arrived_ref, bf16[16,8,128]{2,1,0:T(8,128)(2,1)S(1)} %get-tuple-element.7.mine_ref, ...), custom_call_target="tpu_custom_call" | custom-call | tf_op jit(solution)/shard_map/tile/pallas_call | solution.py:248
  59.6 29.3 %all_to_all.20.returned_ref = bf16[32,64,256]{2,1,0:T(8,128)(2,1)S(1)} all-to-all(bf16[32,64,256]{2,1,0:T(8,128)(2,1)S(1)} %tile.1), channel_id=1, replica_groups={{0,1,15,14,13,12,2,9,10,8,7,6,5,4,3,11,16,17,18,19,20,21,22,23,24,25,26..., dimensions={0} | all-to-all | bytes 2097152 | tf_op jit(solution)/shard_map/all_to_all | solution.py:53
  88.8 1.5 %sum.1 = bf16[16,64,256]{2,1,0:T(8,128)(2,1)S(1)} custom-call(s32[32]{0:T(128)S(1)} %dynamic-slice_bitcast_fusion.slot_ref, bf16[32,64,256]{2,1,0:T(8,128)(2,1)S(1)} %all_to_all.20.returned_ref), custom_call_target="tpu_custom_call" | custom-call | tf_op jit(solution)/shard_map/sum/pallas_call | solution.py:260
  90.3 16.7 %all_to_all.21.sums_ref = bf16[16,64,256]{2,1,0:T(8,128)(2,1)S(1)} all-to-all(bf16[16,64,256]{2,1,0:T(8,128)(2,1)S(1)} %sum.1), channel_id=1, replica_groups={{16,20,6,28,4,22,26,8,12,24,10,14,2,0,30,18},{17,21,7,29,5,23,27,9,13,2..., dimensions={0} | all-to-all | bytes 1048576 | tf_op jit(solution)/shard_map/all_to_all | solution.py:47
  107.1 0.0 copy-done.1
  107.1 1.5 %update.1 = (f32[1024,256]{1,0:T(8,128)}, f32[1024,256]{1,0:T(8,128)}) custom-call(bf16[16,64,256]{2,1,0:T(8,128)(2,1)S(1)} %all_to_all.21.sums_ref, f32[1024,256]{1,0:T(8,128)S(1)} %bitcast.16, f32[1024,256]{1,0:T(8,128)S(1)} %bitcast.17), custom_call_target="tpu_custom_call" | custom-call | tf_op jit(solution)/shard_map/update/pallas_call | solution.py:269
  (7 shorter events, 0.0 us)
Async XLA Ops:
  2.6 22.5 %all-to-all-start = ((bf16[16,136,128]{2,1,0:T(8,128)(2,1)}), bf16[16,136,128]{2,1,0:T(8,128)(2,1)S(1)}, u32[]{:S(2)}, u32[]{:S(2)}) async-start(bf16[16,136,128]{2,1,0:T(8,128)(2,1)} %pack.1), calls=%async_computation | async-start | bytes 1114112 | tf_op jit(solution)/shard_map/all_to_all | solution.py:47
  26.9 28.5 %all-to-all-start.1 = ((bf16[32,128,128]{2,1,0:T(8,128)(2,1)}), bf16[32,128,128]{2,1,0:T(8,128)(2,1)S(1)}, u32[]{:S(2)}, u32[]{:S(2)}) async-start(bf16[32,128,128]{2,1,0:T(8,128)(2,1)} %get-tuple-element.6), calls=%async_computation.1 | async-start | bytes 2097152 | tf_op jit(solution)/shard_map/all_to_all | solution.py:53
  32.6 1.3 %collective-permute-start = (bf16[16,8,128]{2,1,0:T(8,128)(2,1)S(1)}, bf16[16,8,128]{2,1,0:T(8,128)(2,1)S(1)}, u32[]{:S(2)}, u32[]{:S(2)}) collective-permute-start(bf16[16,8,128]{2,1,0:T(8,128)(2,1)S(1)} %get-tuple-element.7.mine_ref), channel_id=1, source_target_pairs={{0,1},{1,0},{2,3},{3,2},{4,5},{5,4},{6,7},{7,6},{8,9},{9,8},{10,11... | collective-permute-start | bytes 98312 | tf_op jit(solution)/shard_map/ppermute | solution.py:246
  55.4 51.7 %copy-start = (f32[1,1024,256]{2,1,0:T(8,128)S(1)}, f32[1,1024,256]{2,1,0:T(8,128)}, u32[]{:S(2)}) copy-start(f32[1,1024,256]{2,1,0:T(8,128)} %param.10) | copy-start | bytes 3145732
  55.4 51.7 %copy-start.1 = (f32[1,1024,256]{2,1,0:T(8,128)S(1)}, f32[1,1024,256]{2,1,0:T(8,128)}, u32[]{:S(2)}) copy-start(f32[1,1024,256]{2,1,0:T(8,128)} %param.11) | copy-start | bytes 3145732

commit v7 on v6

--- a/solution.py
+++ b/solution.py
@@ -14,7 +14,7 @@
 LANES = 128
 
 SPREAD_ORDER = (
-    7, 12, 5, 15, 10, 3, 14, 9, 13, 6, 8, 2, 1, 0, 11, 4,
+    7, 3, 13, 15, 10, 12, 2, 11, 5, 6, 8, 14, 1, 0, 9, 4,
 )
 FETCH_ORDER = (
     0, 8, 16, 24, 4, 12, 19, 28, 1, 9, 17, 25, 29, 21, 13, 5,

time: 109 us -> 109 us (level)
  no operation moved by 1% of the time
where the time goes in v7:
time: 109 us; the launch traced here: 108 us
  blocking collectives  46 us (42%)
  waiting for transfers between devices  31.5 us (29%)
  starting transfers between devices  11.6 us (11%)
  Pallas kernels  10.9 us (10%)
  other arithmetic  4.31 us (4%)
  local copies, waits for them, and re-layouts  3.11 us (3%)
    all_to_all x1, blocking collectives, swap_all(): lax.all_to_all(x, ('blk', 'rep'), split_axis=0, concat_axis=0, tiled=True...  29.3 us
    all_to_all x1, waiting for transfers between devices, swap_all(): lax.all_to_all(x, ('blk', 'rep'), split_axis=0, concat_axis=0, tiled=True...  21.5 us
    all_to_all x1, blocking collectives, swap_chips(): lax.all_to_all(x, 'blk', split_axis=0, concat_axis=0, tiled=True, axis_in...  16.7 us
    all_to_all x1, waiting for transfers between devices, swap_chips(): lax.all_to_all(x, 'blk', split_axis=0, concat_axis=0, tiled=True, axis_in...  8.95 us
    all_to_all x1, starting transfers between devices, swap_chips(): lax.all_to_all(x, 'blk', split_axis=0, concat_axis=0, tiled=True, axis_in...  8.79 us
    pallas_call x1, Pallas kernels, per_device(): pl.pallas_call(functools.partial(tile_kernel, orders), in_specs=[smem] +...  4.19 us
    convert_element_type x1, other arithmetic, per_device(): counts[0].astype(bf16)  2.76 us
    all_to_all x1, starting transfers between devices, swap_all(): lax.all_to_all(x, ('blk', 'rep'), split_axis=0, concat_axis=0, tiled=True...  2.66 us
  transfers between devices with their start and end apart: 3, of which 3 were waited for; matrix products, arithmetic and copies ran while one was open for 7% of the time, Pallas kernels for 0%

profile of v7, /device:TPU:0, one launch (start us, length us, event | category | flops | bytes accessed | tf_op | source)
XLA Modules:
  0.0 108.1 jit_solution(11707982846501757033)
XLA Ops:
  0.6 2.0 %pack.1 = bf16[16,136,128]{2,1,0:T(8,128)(2,1)} custom-call(f32[1024,256]{1,0:T(8,128)} %bitcast.15, bf16[1,1024]{1,0:T(2,128)(2,1)} %margin_ref.1), custom_call_target="tpu_custom_call" | custom-call | tf_op jit(solution)/shard_map/pack/pallas_call | solution.py:220
  2.6 8.8 %all-to-all-start = ((bf16[16,136,128]{2,1,0:T(8,128)(2,1)}), bf16[16,136,128]{2,1,0:T(8,128)(2,1)S(1)}, u32[]{:S(2)}, u32[]{:S(2)}) async-start(bf16[16,136,128]{2,1,0:T(8,128)(2,1)} %pack.1), calls=%async_computation | async-start | bytes 1114112 | tf_op jit(solution)/shard_map/all_to_all | solution.py:47
  11.4 0.7 compare_select_fusion
  12.1 0.1 reshape.7
  12.2 1.4 %gather_fusion = s32[32]{0:T(128)S(1)} fusion(s32[16]{0:T(128)} %constant.6.clone, s32[1024]{0:T(1024)S(1)} %pad_clamp_fusion.2), kind=kCustom, calls=%fused_computation | custom fusion | bytes 384 | tf_op jit(solution)/shard_map/gather | solution.py:213
  13.5 0.8 fusion
  14.3 0.1 fusion.2
  14.4 0.7 gather_fusion.2
  15.1 0.7 gather_fusion.1
  15.8 8.9 %all-to-all-done.held_ref = bf16[16,136,128]{2,1,0:T(8,128)(2,1)S(1)} async-done(((bf16[16,136,128]{2,1,0:T(8,128)(2,1)}), bf16[16,136,128]{2,1,0:T(8,128)(2,1)S(1)}, u32[]{:S(2)}, u32[]{:S(2)}) %all-to-all-start) | async-done | bytes 557088 | tf_op jit(solution)/shard_map/all_to_all | solution.py:47
  24.7 1.8 %pick.1 = (bf16[32,128,128]{2,1,0:T(8,128)(2,1)}, bf16[16,8,128]{2,1,0:T(8,128)(2,1)S(1)}) custom-call(s32[32]{0:T(128)S(1)} %dynamic-slice_bitcast_fusion.slot_ref, bf16[16,136,128]{2,1,0:T(8,128)(2,1)S(1)} %all-to-all-done.held_ref), custom_call_target="tpu_custom_call" | custom-call | tf_op jit(solution)/shard_map/pick/pallas_call | solution.py:234
  26.5 2.7 %all-to-all-start.1 = ((bf16[32,128,128]{2,1,0:T(8,128)(2,1)}), bf16[32,128,128]{2,1,0:T(8,128)(2,1)S(1)}, u32[]{:S(2)}, u32[]{:S(2)}) async-start(bf16[32,128,128]{2,1,0:T(8,128)(2,1)} %get-tuple-element.6), calls=%async_computation.1 | async-start | bytes 2097152 | tf_op jit(solution)/shard_map/all_to_all | solution.py:53
  29.2 0.2 dynamic-slice_reduce_fusion
  29.4 2.8 %convert_bitcast_fusion.counts_ref = bf16[1024,1024]{1,0:T(8,128)(2,1)S(1)} fusion(s32[1,1024,1024]{2,1,0:T(8,128)} %param.7), kind=kLoop, calls=%fused_computation.3 | loop fusion | flops 1048576 | bytes 6291456 | tf_op jit(solution)/shard_map/convert_element_type | solution.py:258
  32.2 0.2 collective-permute-start
  32.3 0.1 pad_add_fusion.1.place_ref
  32.4 1.0 collective-permute-done.other_ref
  33.4 21.5 %all-to-all-done.1.arrived_ref = bf16[32,128,128]{2,1,0:T(8,128)(2,1)S(1)} async-done(((bf16[32,128,128]{2,1,0:T(8,128)(2,1)}), bf16[32,128,128]{2,1,0:T(8,128)(2,1)S(1)}, u32[]{:S(2)}, u32[]{:S(2)}) %all-to-all-start.1) | async-done | bytes 1048608 | tf_op jit(solution)/shard_map/all_to_all | solution.py:53
  54.9 4.2 %tile.1 = bf16[32,64,256]{2,1,0:T(8,128)(2,1)S(1)} custom-call(s32[3]{0:T(128)S(1)} %pad_add_fusion.1.place_ref, bf16[1024,1024]{1,0:T(8,128)(2,1)S(1)} %convert_bitcast_fusion.counts_ref, bf16[32,128,128]{2,1,0:T(8,128)(2,1)S(1)} %all-to-all-done.1.arrived_ref, bf16[16,8,128]{2,1,0:T(8,128)(2,1)S(1)} %get-tuple-element.7.mine_ref, ...), custom_call_target="tpu_custom_call" | custom-call | tf_op jit(solution)/shard_map/tile/pallas_call | solution.py:248
  59.1 29.3 %all_to_all.20.returned_ref = bf16[32,64,256]{2,1,0:T(8,128)(2,1)S(1)} all-to-all(bf16[32,64,256]{2,1,0:T(8,128)(2,1)S(1)} %tile.1), channel_id=1, replica_groups={{0,1,15,14,13,12,2,9,10,8,7,6,5,4,3,11,16,17,18,19,20,21,22,23,24,25,26..., dimensions={0} | all-to-all | bytes 2097152 | tf_op jit(solution)/shard_map/all_to_all | solution.py:53
  88.4 1.5 %sum.1 = bf16[16,64,256]{2,1,0:T(8,128)(2,1)S(1)} custom-call(s32[32]{0:T(128)S(1)} %dynamic-slice_bitcast_fusion.slot_ref, bf16[32,64,256]{2,1,0:T(8,128)(2,1)S(1)} %all_to_all.20.returned_ref), custom_call_target="tpu_custom_call" | custom-call | tf_op jit(solution)/shard_map/sum/pallas_call | solution.py:260
  89.9 16.7 %all_to_all.21.sums_ref = bf16[16,64,256]{2,1,0:T(8,128)(2,1)S(1)} all-to-all(bf16[16,64,256]{2,1,0:T(8,128)(2,1)S(1)} %sum.1), channel_id=1, replica_groups={{16,20,6,28,4,22,26,8,12,24,10,14,2,0,30,18},{17,21,7,29,5,23,27,9,13,2..., dimensions={0} | all-to-all | bytes 1048576 | tf_op jit(solution)/shard_map/all_to_all | solution.py:47
  106.6 0.0 copy-done
  106.6 1.5 %update.1 = (f32[1024,256]{1,0:T(8,128)}, f32[1024,256]{1,0:T(8,128)}) custom-call(bf16[16,64,256]{2,1,0:T(8,128)(2,1)S(1)} %all_to_all.21.sums_ref, f32[1024,256]{1,0:T(8,128)S(1)} %bitcast.16, f32[1024,256]{1,0:T(8,128)S(1)} %bitcast.17), custom_call_target="tpu_custom_call" | custom-call | tf_op jit(solution)/shard_map/update/pallas_call | solution.py:269
  (7 shorter events, 0.0 us)
Async XLA Ops:
  2.6 22.1 %all-to-all-start = ((bf16[16,136,128]{2,1,0:T(8,128)(2,1)}), bf16[16,136,128]{2,1,0:T(8,128)(2,1)S(1)}, u32[]{:S(2)}, u32[]{:S(2)}) async-start(bf16[16,136,128]{2,1,0:T(8,128)(2,1)} %pack.1), calls=%async_computation | async-start | bytes 1114112 | tf_op jit(solution)/shard_map/all_to_all | solution.py:47
  26.5 28.4 %all-to-all-start.1 = ((bf16[32,128,128]{2,1,0:T(8,128)(2,1)}), bf16[32,128,128]{2,1,0:T(8,128)(2,1)S(1)}, u32[]{:S(2)}, u32[]{:S(2)}) async-start(bf16[32,128,128]{2,1,0:T(8,128)(2,1)} %get-tuple-element.6), calls=%async_computation.1 | async-start | bytes 2097152 | tf_op jit(solution)/shard_map/all_to_all | solution.py:53
  32.2 1.3 %collective-permute-start = (bf16[16,8,128]{2,1,0:T(8,128)(2,1)S(1)}, bf16[16,8,128]{2,1,0:T(8,128)(2,1)S(1)}, u32[]{:S(2)}, u32[]{:S(2)}) collective-permute-start(bf16[16,8,128]{2,1,0:T(8,128)(2,1)S(1)} %get-tuple-element.7.mine_ref), channel_id=1, source_target_pairs={{0,1},{1,0},{2,3},{3,2},{4,5},{5,4},{6,7},{7,6},{8,9},{9,8},{10,11... | collective-permute-start | bytes 98312 | tf_op jit(solution)/shard_map/ppermute | solution.py:246
  54.9 51.7 %copy-start = (f32[1,1024,256]{2,1,0:T(8,128)S(1)}, f32[1,1024,256]{2,1,0:T(8,128)}, u32[]{:S(2)}) copy-start(f32[1,1024,256]{2,1,0:T(8,128)} %param.10) | copy-start | bytes 3145732
  54.9 51.7 %copy-start.1 = (f32[1,1024,256]{2,1,0:T(8,128)S(1)}, f32[1,1024,256]{2,1,0:T(8,128)}, u32[]{:S(2)}) copy-start(f32[1,1024,256]{2,1,0:T(8,128)} %param.11) | copy-start | bytes 3145732
